TPU v7x, 512 devices: a whole 4x4x16 slice. The times are simulated.
512 devices in a mesh: tile: 16 (over z_lo, core), wide: 32 (over y, z_hi, x).
Axes of the slice: x: 4, y: 4, z: 16 (z_hi: 2, z_lo: 8; z = z_hi * 8 + z_lo), core: 2. Of those that a mesh axis runs over, the one named last changes fastest.
Arguments:
- coefficients: bfloat16 [1536, 1536], P('tile', 'wide'), may hold values from -6 to 6
- integrals: bfloat16 [400, 400], replicated, may hold values from -0.0390625 to 0.0390625
- targets: int32 [110, 1536], replicated, may hold values from 0 to 1535, as said below
- orbital_pairs: int32 [110, 1536], replicated, may hold values from 0 to 399, as said below
- phases: int32 [110, 1536], replicated, may hold values from -1 to 1, as said below
Outputs:
- sigma: float32 [1536, 1536], P('tile', 'wide')
Inputs may be any that keep to these rules, and one draw needn't show every extreme that they name: targets[e, b] is the string that excitation e of string b leads to; the entries e = k * (11) are b itself. `orbital_pairs`: each column holds 110 distinct pairs p * 20 + q, q one of the string's 10 occupied orbitals and p either q or an empty orbital. `phases`: each entry is 1 or -1; 1 where the target is the string itself.
All inputs are finite; a program needn't handle non-finite values.
Results may differ from a plain program's by a relative error of at most 0.0029.
Values may be sent and summed in bfloat16 or wider, within the bound.
A program may use at most 64 MiB of HBM per device.

v0:
```python
import jax
import jax.numpy as jnp
from jax import lax
from jax.sharding import PartitionSpec as P


def pair_onehot(pair_rows, npairs):
    return (pair_rows[:, :, None] == jnp.arange(npairs, dtype=jnp.int32)[None, None, :]).astype(
        jnp.bfloat16
    )


def couple(spread, integrals):
    return jnp.einsum("abq,pq->abp", spread, integrals, preferred_element_type=jnp.float32).astype(
        jnp.bfloat16
    )


def string_slice(table, start, count):
    return lax.dynamic_slice_in_dim(table, start, count, 1).T


def per_device(coefficients, integrals, targets, orbital_pairs, phases):
    row_count, col_count = coefficients.shape
    npairs = integrals.shape[0]
    wide_start = lax.axis_index("wide") * col_count
    own_targets = string_slice(targets, wide_start, col_count)
    own_pairs = string_slice(orbital_pairs, wide_start, col_count)
    own_phases = string_slice(phases, wide_start, col_count)
    own_hot = pair_onehot(own_pairs, npairs)
    own_sign = own_phases.astype(jnp.bfloat16)
    own_float = own_phases.astype(jnp.float32)
    flat_targets = own_targets.reshape(-1)
    row_block = lax.all_gather(coefficients, "wide", axis=1, tiled=True)
    total_cols = row_block.shape[1]
    values = row_block[:, own_targets] * own_sign[None]
    spread = jnp.einsum("abe,bep->abp", values, own_hot, preferred_element_type=jnp.float32).astype(
        jnp.bfloat16
    )
    coupled = couple(spread, integrals)
    picked = (
        jnp.einsum("abp,bep->abe", coupled, own_hot, preferred_element_type=jnp.float32)
        * own_float[None]
    )
    partial_value = (
        jnp.zeros((row_count, total_cols), jnp.float32)
        .at[:, flat_targets]
        .add(picked.reshape(row_count, -1))
    )
    mirrored = lax.all_to_all(row_block, "tile", split_axis=1, concat_axis=0, tiled=True)
    values_t = mirrored[own_targets] * own_sign[:, :, None]
    spread_t = jnp.einsum(
        "bea,bep->abp", values_t, own_hot, preferred_element_type=jnp.float32
    ).astype(jnp.bfloat16)
    coupled_t = couple(spread_t, integrals)
    picked_t = (
        jnp.einsum("abp,bep->bea", coupled_t, own_hot, preferred_element_type=jnp.float32)
        * own_float[:, :, None]
    )
    flipped = (
        jnp.zeros((total_cols, row_count), jnp.float32)
        .at[flat_targets]
        .add(picked_t.reshape(-1, row_count))
    )
    partial_value = partial_value + lax.all_to_all(
        flipped, "tile", split_axis=0, concat_axis=1, tiled=True
    )
    sigma = lax.psum_scatter(partial_value, "wide", scatter_dimension=1, tiled=True)
    return sigma


def solution(mesh):
    in_specs = (P("tile", "wide"), P(), P(), P(), P())
    out_specs = P("tile", "wide")
    return jax.shard_map(
        per_device, mesh=mesh, in_specs=in_specs, out_specs=out_specs, check_vma=False
    )
```

profile of v0, /device:TPU:1, one launch (start us, length us, event | category | flops | bytes accessed | tf_op | source)
XLA Modules:
  0.0 652.5 jit_solution(14605724408600377791)
XLA Ops:
  6.5 0.0 copy-start
  6.5 153.0 %all_gather.3 = bf16[96,1536]{0,1:T(8,128)(2,1)S(1)} all-gather(bf16[96,48]{0,1:T(8,128)(2,1)} %param.5), channel_id=1, replica_groups=mesh['tile'=16,'wide'=32] {'wide'}, dimensions={1}, use_global_device_ids=true | all-gather | bytes 304128 | tf_op jit(solution)/shard_map/all_gather | solution.py:34
  159.6 0.9 copy.40
  160.5 19.6 %all-to-all-start = ((bf16[96,16,96]{2,0,1:T(8,128)(2,1)}), bf16[96,16,96]{2,0,1:T(8,128)(2,1)S(1)}, u32[]{:S(2)}, u32[]{:S(2)}) async-start(bf16[96,16,96]{2,0,1:T(8,128)(2,1)} %copy.40), calls=%async_computation | async-start | bytes 786432 | tf_op jit(solution)/shard_map/all_to_all | solution.py:50
  180.1 1.0 compare_select_fusion
  181.1 0.1 copy.38
  181.2 0.1 reshape.48
  181.3 1.1 convert_bitcast_fusion
  182.4 0.1 copy.39
  182.4 0.1 copy.41
  182.5 0.1 reshape.53
  182.7 10.5 %gather_fusion.1 = bf16[5280,96]{1,0:T(8,128)(2,1)S(1)} fusion(bf16[96,1536]{0,1:T(8,128)(2,1)S(1)} %all_gather.3, s32[6144]{0:T(1024)S(1)} %pad_clamp_fusion), kind=kCustom, calls=%fused_computation.1 | custom fusion | bytes 2048640 | tf_op jit(solution)/shard_map/gather | solution.py:36
  193.2 1.8 copy.50
  195.0 3.6 reshape.64
  198.6 0.1 copy.43
  198.7 0.1 copy.45
  198.7 0.1 fusion.30
  198.8 0.0 copy-start.3
  198.8 2.8 all-to-all-done
  201.7 10.5 %gather_fusion = bf16[5280,96]{1,0:T(8,128)(2,1)S(1)} fusion(bf16[1536,96]{1,0:T(8,128)(2,1)S(1)} %bitcast.40, s32[6144]{0:T(1024)S(1)} %pad_clamp_fusion), kind=kCustom, calls=%fused_computation | custom fusion | bytes 2048640 | tf_op jit(solution)/shard_map/gather | solution.py:51
  212.2 1.8 copy.42
  214.0 3.6 reshape.52
  217.6 1.6 multiply_bitcast_fusion.1
  219.2 0.0 copy-done
  219.2 7.6 %fusion.10 = bf16[96,48,400]{2,0,1:T(8,128)(2,1)} fusion(s32[48,110]{1,0:T(8,128)S(1)} %copy.39, bf16[48,110,96]{1,0,2:T(8,128)(2,1)} %get-tuple-element.10, bf16[400,400]{1,0:T(8,128)(2,1)S(1)} %copy-done), kind=kOutput, calls=%fused_computation.15 | convolution fusion | flops 1884019200 | bytes 5041280 | tf_op jit(solution)/shard_map/abq,pq->abp/dot_general | solution.py:14
  226.8 6.2 fusion.16
  233.0 2.3 copy.54
  235.2 1.6 reshape.88
  236.9 0.0 copy-done.3
  236.9 0.0 copy-start.2
  236.9 31.2 %scatter_custom_fusion = f32[1536,96]{1,0:T(8,128)S(1)} fusion(s32[5280]{0:T(1024)S(1)} %fusion.30, f32[5280,96]{1,0:T(8,128)} %reshape.88, f32[]{:T(128)} %constant.5.clone.1), kind=kCustom, calls=%fused_computation.29 | custom fusion | flops 506880 | bytes 590336 | tf_op jit(solution)/shard_map/scatter-add | solution.py:63
  268.1 1.2 copy.49
  269.2 7.1 %all-to-all-start.1 = ((f32[16,96,96]{1,2,0:T(8,128)}), f32[16,96,96]{1,2,0:T(8,128)S(1)}, u32[]{:S(2)}, u32[]{:S(2)}) async-start(f32[16,96,96]{1,2,0:T(8,128)} %copy.49), calls=%async_computation.1 | async-start | bytes 1572864 | tf_op jit(solution)/shard_map/all_to_all | solution.py:65
  276.3 0.0 reduce-scatter.2.cloned.1.call-start
  276.4 0.0 copy-done.2
  276.4 6.6 %fusion.8 = bf16[96,48,400]{2,0,1:T(8,128)(2,1)} fusion(s32[48,110]{1,0:T(8,128)S(1)} %copy.39, bf16[96,48,110]{2,1,0:T(8,128)(2,1)S(1)} %copy-done.2, bf16[400,400]{1,0:T(8,128)(2,1)S(1)} %copy-done), kind=kOutput, calls=%fused_computation.13 | convolution fusion | flops 1884019200 | bytes 5041280 | tf_op jit(solution)/shard_map/abq,pq->abp/dot_general | solution.py:14
  283.0 4.7 multiply_bitcast_fusion
  287.7 1.4 copy.52
  289.1 2.0 reshape.76
  291.1 0.0 copy-start.4
  291.1 3.2 copy.53
  294.3 17.4 %all-to-all-done.1 = f32[16,96,96]{1,2,0:T(8,128)S(1)} async-done(((f32[16,96,96]{1,2,0:T(8,128)}), f32[16,96,96]{1,2,0:T(8,128)S(1)}, u32[]{:S(2)}, u32[]{:S(2)}) %all-to-all-start.1) | async-done | bytes 589856 | tf_op jit(solution)/shard_map/all_to_all | solution.py:65
  311.6 0.0 copy-done.4
  311.6 31.2 %scatter_fusion = f32[96,1536]{0,1:T(8,128)S(1)} fusion(f32[96,1536]{0,1:T(8,128)S(1)} %bitcast.39, s32[5280]{0:T(1024)S(1)} %copy-done.4, f32[5280,96]{1,0:T(8,128)} %copy.53), kind=kCustom, calls=%fused_computation.3 | custom fusion | flops 506880 | bytes 6103680 | tf_op jit(solution)/shard_map/scatter-add | solution.py:48
  342.8 0.0 copy-start.1
  342.9 0.9 copy-done.1
  343.7 0.0 reduce-scatter.2.cloned.1.call-update
  343.8 301.9 %reduce-scatter.2.cloned.1.call-done = f32[96,48]{0,1:T(8,128)} async-done(((f32[96,1536]{0,1:T(8,128)}), f32[96,48]{0,1:T(8,128)}) %reduce-scatter.2.cloned.1.call-update) | async-done | bytes 18448 | tf_op jit(solution)/shard_map/reduce_scatter | solution.py:68
  (1 shorter events, 0.0 us)
Async XLA Ops:
  6.5 212.7 %copy-start = (bf16[400,400]{1,0:T(8,128)(2,1)S(1)}, bf16[400,400]{1,0:T(8,128)(2,1)}, u32[]{:S(2)}) copy-start(bf16[400,400]{1,0:T(8,128)(2,1)} %param.6) | copy-start | bytes 960004
  160.5 41.2 %all-to-all-start = ((bf16[96,16,96]{2,0,1:T(8,128)(2,1)}), bf16[96,16,96]{2,0,1:T(8,128)(2,1)S(1)}, u32[]{:S(2)}, u32[]{:S(2)}) async-start(bf16[96,16,96]{2,0,1:T(8,128)(2,1)} %copy.40), calls=%async_computation | async-start | bytes 786432 | tf_op jit(solution)/shard_map/all_to_all | solution.py:50
  198.8 38.0 %copy-start.3 = (s32[5280]{0:T(1024)}, s32[5280]{0:T(1024)S(1)}, u32[]{:S(2)}) copy-start(s32[5280]{0:T(1024)S(1)} %fusion.30) | copy-start | bytes 63364
  236.9 39.5 %copy-start.2 = (bf16[96,48,110]{2,1,0:T(8,128)(2,1)S(1)}, bf16[96,48,110]{2,1,0:T(8,128)(2,1)}, u32[]{:S(2)}) copy-start(bf16[96,48,110]{2,1,0:T(8,128)(2,1)} %get-tuple-element.9) | copy-start | bytes 3041284
  269.2 42.4 %all-to-all-start.1 = ((f32[16,96,96]{1,2,0:T(8,128)}), f32[16,96,96]{1,2,0:T(8,128)S(1)}, u32[]{:S(2)}, u32[]{:S(2)}) async-start(f32[16,96,96]{1,2,0:T(8,128)} %copy.49), calls=%async_computation.1 | async-start | bytes 1572864 | tf_op jit(solution)/shard_map/all_to_all | solution.py:65
  276.3 369.3 %reduce-scatter.2.cloned.1.call-start = ((), (), s32[]{:S(2)}) async-start(), calls=%async_computation.3 | async-start | bytes 811008 | tf_op jit(solution)/shard_map/reduce_scatter | solution.py:68
  291.1 20.6 %copy-start.4 = (s32[5280]{0:T(1024)S(1)}, s32[5280]{0:T(1024)}, u32[]{:S(2)}) copy-start(s32[5280]{0:T(1024)} %copy-done.3) | copy-start | bytes 63364
  342.8 0.9 copy-start.1
Sparse Core Ops, SparseCore 0:
  343.9 301.6 reduce-scatter.1
where the time goes:
time: 653 us; the launch traced here: 652 us
  waiting for transfers between devices  322 us (49%)
  blocking collectives  153 us (23%)
  other arithmetic  66.1 us (10%)
  local copies, waits for them, and re-layouts  45.9 us (7%)
  starting transfers between devices  26.7 us (4%)
  matrix products  25.1 us (4%)
  between operations  13.5 us (2%)
    reduce_scatter x1, waiting for transfers between devices, per_device(): lax.psum_scatter(partial_value, 'wide', scatter_dimension=1, tiled=True)  302 us
    all_gather x1, blocking collectives, per_device(): row_block = lax.all_gather(coefficients, 'wide', axis=1, tiled=True)  153 us
    scatter-add x1, other arithmetic, per_device(): partial_value = jnp.zeros((row_count, total_cols), jnp.float32).at[:, fla...  31.2 us
    scatter-add x1, other arithmetic, per_device(): flipped = jnp.zeros((total_cols, row_count), jnp.float32).at[flat_targets...  31.2 us
    all_to_all x1, starting transfers between devices, per_device(): lax.all_to_all(row_block, 'tile', split_axis=1, concat_axis=0, tiled=True)  19.6 us
    all_to_all x1, waiting for transfers between devices, per_device(): lax.all_to_all(flipped, 'tile', split_axis=0, concat_axis=1, tiled=True)  17.4 us
    gather x3, local copies, waits for them, and re-layouts, per_device(): values = row_block[:, own_targets] * own_sign[None]  15.9 us
    gather x3, local copies, waits for them, and re-layouts, per_device(): values_t = mirrored[own_targets] * own_sign[:, :, None]  15.9 us
  transfers between devices with their start and end apart: 3, of which 3 were waited for; matrix products, arithmetic and copies ran while one was open for 6% of the time, Pallas kernels for 0%

commit v1 on v0

v1 whole, which is shorter than its diff:
```python
import functools
import types

import jax
import jax.numpy as jnp
from jax import lax
from jax.experimental import pallas as pl
from jax.experimental.pallas import tpu as pltpu
from jax.sharding import PartitionSpec as P

LANES = 128
MESH = pl.DeviceIdType.MESH


def plan_of(mesh, coef_shape, exc_shape, pair_count):
    tiles, wides = mesh.shape["tile"], mesh.shape["wide"]
    xs = 4 if wides == 32 else 2
    ys = wides // (2 * xs)
    strings = coef_shape[0]
    rows, cols = strings // tiles, strings // wides
    chunks = tiles // 4
    chunk = cols // chunks
    return types.SimpleNamespace(
        tiles=tiles,
        wides=wides,
        xs=xs,
        ys=ys,
        plane=xs * ys * 2,
        strings=strings,
        rows=rows,
        cols=cols,
        quad=tiles // 4,
        chunks=chunks,
        chunk=chunk,
        chunk_pad=-(-chunk // 16) * 16,
        sets=xs * ys // 2,
        own=strings // (xs * ys * 2),
        exc=exc_shape[0],
        pairs=pair_count,
        pair_pad=-(-pair_count // LANES) * LANES,
        step=8,
    )


def kernel(n, coef, integ, tgt, prs, phs, out, raw, tabs, g_pad, c_pad, first, hold, gath, xt, x_all,
           t_all, w_all, u_all, part, rs_out, rs_in, fin, fin_in, s_tab, s1, r1, s2, r2, s3, r3, s4, r4):
    bf16, f32 = jnp.bfloat16, jnp.float32
    slot_rows = n.cols + n.quad * n.chunk_pad
    tile, wide = lax.axis_index("tile"), lax.axis_index("wide")
    core, zl = lax.rem(tile, 2), tile // 2
    x, zh, y = lax.rem(wide, n.xs), lax.rem(wide // n.xs, 2), wide // (2 * n.xs)
    me = (y * n.xs + x) * 2 + core

    def device(xx, yy, zzh, zzl, cc):
        return (zzl * 2 + cc, (yy * 2 + zzh) * n.xs + xx)

    def plane_device(p):
        return device(lax.rem(p // 2, n.xs), p // (2 * n.xs), zh, zl, lax.rem(p, 2))

    def peer(d):
        return lax.rem(me + d, n.plane)

    def source(d):
        return lax.rem(me + n.plane - d, n.plane)

    def flip(a, b):
        return lax.rem(a + b, 2)

    crosses = zh != core
    far = device(x, y, 1 - zh, zl, 1 - core)
    my_quad, my_slot = tile // n.quad, lax.rem(tile, n.quad)
    to_x = (x // 2) * 2 + flip(lax.rem(x, 2), my_quad // 2)
    to_core = lax.rem(my_quad, 2)

    def target(m):
        zz = 2 * m + lax.rem(x, 2)
        is_me = (to_x == x) & (to_core == core) & (zz == zl)
        return device(to_x, y, zh, zz, to_core), is_me

    from_x = (x // 2) * 2 + lax.rem(zl, 2)
    held_quad = 2 * flip(lax.rem(x, 2), lax.rem(zl, 2)) + core

    def giver(k):
        t = held_quad * n.quad + k
        is_me = (from_x == x) & (t == tile)
        return device(from_x, y, zh, t // 2, lax.rem(t, 2)), is_me

    held_chunk = zl // 2

    start = me * n.own
    window = jnp.minimum(start // LANES * LANES, n.strings - 2 * LANES)
    window = pl.multiple_of(window, LANES)
    loads = [
        pltpu.make_async_copy(
            ref.at[:, pl.ds(window, 2 * LANES)], raw.at[i], s_tab.at[i]
        )
        for i, ref in enumerate((tgt, prs, phs))
    ]
    for load in loads:
        load.start()

    barrier = pltpu.get_barrier_semaphore()

    def greet(d, carry):
        pl.semaphore_signal(barrier, inc=1, device_id=plane_device(peer(d)), device_id_type=MESH)
        return carry

    lax.fori_loop(1, n.plane, greet, 0)
    for m in range(n.chunks):
        where_to, is_me = target(m)

        @pl.when(jnp.logical_not(is_me))
        def _():
            pl.semaphore_signal(barrier, inc=1, device_id=where_to, device_id_type=MESH)

    for k in range(n.quad):
        whose, is_me = giver(k)

        @pl.when(jnp.logical_not(is_me))
        def _():
            pl.semaphore_signal(barrier, inc=1, device_id=whose, device_id_type=MESH)

    @pl.when(crosses)
    def _():
        pl.semaphore_signal(barrier, inc=1, device_id=far, device_id_type=MESH)

    c_pad[...] = jnp.zeros_like(c_pad)
    c_pad[0:n.rows, 0:n.cols] = coef[...].astype(f32)
    block_t = c_pad[...].T
    first[0:n.cols] = block_t[0:n.cols].astype(bf16)
    for m in range(n.chunks):
        piece = block_t[m * n.chunk : m * n.chunk + n.chunk_pad]
        at = n.cols + m * n.chunk_pad
        first[at : at + n.chunk_pad] = piece.astype(bf16)

    g_pad[...] = jnp.zeros_like(g_pad)
    g_pad[0:n.pairs, 0:n.pairs] = integ[...]
    tabs[...] = jnp.zeros_like(tabs)
    for load in loads:
        load.wait()
    tabs[:, 0 : n.exc] = raw[...]

    itself = jnp.int32(0)
    for m in range(n.chunks):
        itself = itself + target(m)[1].astype(jnp.int32)
    expected = n.plane - 1 + n.chunks + n.quad - 2 * itself + crosses.astype(jnp.int32)
    pl.semaphore_wait(barrier, expected)

    def piece_rows(k):
        return pl.ds(pl.multiple_of(n.cols + k * n.chunk_pad, 16), n.chunk_pad)

    swap = pltpu.make_async_remote_copy(
        src_ref=first.at[pl.ds(0, n.cols)],
        dst_ref=hold.at[pl.ds(0, n.cols)],
        send_sem=s1.at[0],
        recv_sem=r1.at[0],
        device_id=far,
        device_id_type=MESH,
    )

    def give(m):
        return pltpu.make_async_remote_copy(
            src_ref=first.at[piece_rows(m)],
            dst_ref=hold.at[piece_rows(my_slot)],
            send_sem=s1.at[1 + m],
            recv_sem=r1.at[1 + my_slot],
            device_id=target(m)[0],
            device_id_type=MESH,
        )

    def take(k):
        return pltpu.make_async_remote_copy(
            src_ref=first.at[piece_rows(0)],
            dst_ref=hold.at[piece_rows(k)],
            send_sem=s1.at[1],
            recv_sem=r1.at[1 + k],
            device_id=giver(k)[0],
            device_id_type=MESH,
        )

    @pl.when(crosses)
    def _():
        swap.start()

    @pl.when(jnp.logical_not(crosses))
    def _():
        hold[0 : n.cols] = first[0 : n.cols]

    for m in range(n.chunks):
        is_me = target(m)[1]

        @pl.when(jnp.logical_not(is_me))
        def _():
            give(m).start()

        @pl.when(is_me)
        def _():
            hold[piece_rows(my_slot)] = first[piece_rows(m)]

    offset = start - window
    lane = lax.broadcasted_iota(jnp.int32, (LANES, LANES), 1).astype(f32).astype(bf16)
    one, zero = jnp.ones((), bf16), jnp.zeros((), bf16)

    def spread_col(col):
        return jnp.broadcast_to(col, (LANES, LANES)).astype(bf16)

    def build(it, carry):
        shift = lax.rem(2 * 2 * LANES - offset - it * n.step, 2 * LANES)
        t = pltpu.roll(tabs[0], shift, 1)[:, 0:LANES]
        q = pltpu.roll(tabs[1], shift, 1)[:, 0:LANES]
        s = pltpu.roll(tabs[2], shift, 1)[:, 0:LANES].astype(f32)
        t_hi, t_lo = (t // LANES).astype(f32), lax.rem(t, LANES).astype(f32)
        q_hi, q_lo = (q // LANES).astype(f32), lax.rem(q, LANES).astype(f32)
        for u in range(n.step):
            b = it * n.step + u
            rows = pl.ds(pl.multiple_of(b * LANES, LANES), LANES)
            hi, lo = spread_col(t_hi[:, u : u + 1]), spread_col(t_lo[:, u : u + 1])
            hot = jnp.where(lo == lane, one, zero)
            for kt in range(n.strings // LANES):
                t_all[rows, kt * LANES : (kt + 1) * LANES] = jnp.where(hi == kt, hot, zero)
            hi, lo = spread_col(q_hi[:, u : u + 1]), spread_col(q_lo[:, u : u + 1])
            sign = spread_col(s[:, u : u + 1])
            hot = jnp.where(lo == lane, sign, zero)
            signed = jnp.concatenate(
                [jnp.where(hi == kt, hot, zero) for kt in range(n.pair_pad // LANES)], axis=1
            )
            picked = lax.dot_general(
                signed, g_pad[...], (((1,), (1,)), ((), ())), preferred_element_type=f32
            ).astype(bf16)
            w_all[b] = lax.dot_general(
                picked, signed, (((1,), (1,)), ((), ())), preferred_element_type=f32
            ).astype(bf16)
        return carry

    builds = n.own // n.step
    early = max(1, builds // 3)
    lax.fori_loop(0, early, build, 0)

    @pl.when(crosses)
    def _():
        swap.wait_recv()

    for k in range(n.quad):

        @pl.when(jnp.logical_not(giver(k)[1]))
        def _():
            take(k).wait_recv()

    def share(d, into):
        return pltpu.make_async_remote_copy(
            src_ref=hold,
            dst_ref=gath.at[into],
            send_sem=s2.at[d],
            recv_sem=r2.at[d],
            device_id=plane_device(peer(d)),
            device_id_type=MESH,
        )

    def start_share(d, carry):
        share(d, me).start()
        return carry

    lax.fori_loop(1, n.plane, start_share, 0)
    gath[me] = hold[...]

    lax.fori_loop(early, builds, build, 0)

    def wait_share(d, carry):
        share(d, source(d)).wait_recv()
        return carry

    lax.fori_loop(1, n.plane, wait_share, 0)

    for w in range(n.plane):
        yy, cc, xx = w // (2 * n.xs), w // n.xs % 2, w % n.xs
        p = (yy * n.xs + xx) * 2 + cc
        xt[w * n.cols : (w + 1) * n.cols] = gath[p, 0 : n.cols].astype(f32)
    for kt in range(n.strings // LANES):
        at = slice(kt * LANES, (kt + 1) * LANES)
        x_all[0:LANES, at] = xt[at].T.astype(bf16)

    lane_i = lax.broadcasted_iota(jnp.int32, (LANES, LANES), 1)
    zl_odd = lax.rem(zl, 2)

    def alpha_piece(t):
        quad, slot = t // n.quad, t % n.quad
        at = n.cols + slot * n.chunk_pad
        pieces = []
        for s in range(n.sets):
            yy, xh = s // (n.xs // 2), s % (n.xs // 2)
            xx = 2 * xh + flip(zl_odd, quad // 2)
            p = (yy * n.xs + xx) * 2 + quad % 2
            pieces.append(gath[p, at : at + n.chunk_pad].astype(f32))
        short = LANES - n.sets * n.chunk_pad
        if short:
            pieces.append(jnp.zeros((short, LANES), f32))
        return jnp.concatenate(pieces, axis=0)

    for four in range(n.tiles // 4):
        p0, p1, p2, p3 = (alpha_piece(4 * four + i) for i in range(4))
        p1, p2, p3 = pltpu.roll(p1, 96, 1), pltpu.roll(p2, 64, 1), pltpu.roll(p3, 32, 1)
        tiles3 = (
            jnp.where(lane_i < 96, p0, p1),
            jnp.where(lane_i < 64, p1, p2),
            jnp.where(lane_i < 32, p2, p3),
        )
        for i, value in enumerate(tiles3):
            at = (3 * four + i) * LANES
            x_all[LANES : 2 * LANES, at : at + LANES] = value.astype(bf16)

    def couple(it, carry):
        rows = pl.ds(pl.multiple_of(it * 2 * LANES, 2 * LANES), 2 * LANES)
        v = lax.dot_general(
            x_all[...], t_all[rows, :], (((1,), (1,)), ((), ())), preferred_element_type=f32
        ).astype(bf16)
        for u in range(2):
            value = jnp.dot(
                v[:, u * LANES : (u + 1) * LANES], w_all[it * 2 + u], preferred_element_type=f32
            )
            at = pl.ds(pl.multiple_of((it * 2 + u) * LANES, LANES), LANES)
            u_all[:, at] = value.astype(bf16)
        return carry

    lax.fori_loop(0, n.own // 2, couple, 0)

    width = 3 * LANES

    def scatter(it, carry):
        at = pl.ds(pl.multiple_of(it * width, LANES), width)
        part[:, at] = jnp.dot(u_all[...], t_all[:, at], preferred_element_type=f32)
        return carry

    lax.fori_loop(0, n.strings // width, scatter, 0)

    for kt in range(n.strings // LANES):
        at = slice(kt * LANES, (kt + 1) * LANES)
        xt[at] = part[0:LANES, at].T
    for w in range(n.plane):
        yy, cc, xx = w // (2 * n.xs), w // n.xs % 2, w % n.xs
        p = (yy * n.xs + xx) * 2 + cc
        rs_out[p, 0 : n.cols] = xt[w * n.cols : (w + 1) * n.cols].astype(bf16)
    for four in range(n.tiles // 4):
        t0, t1, t2 = (
            part[LANES : 2 * LANES, (3 * four + i) * LANES : (3 * four + i + 1) * LANES]
            for i in range(3)
        )
        roll = functools.partial(pltpu.roll, axis=1)
        values = (
            t0,
            jnp.where(lane_i < 32, roll(t0, 32), roll(t1, 32)),
            jnp.where(lane_i < 64, roll(t1, 64), roll(t2, 64)),
            roll(t2, 96),
        )
        for i, value in enumerate(values):
            t = 4 * four + i
            quad, slot = t // n.quad, t % n.quad
            at = n.cols + slot * n.chunk_pad
            value = value.astype(bf16)
            for s in range(n.sets):
                yy, xh = s // (n.xs // 2), s % (n.xs // 2)
                xx = 2 * xh + flip(zl_odd, quad // 2)
                p = (yy * n.xs + xx) * 2 + quad % 2
                rs_out[p, at : at + n.chunk_pad] = value[s * n.chunk_pad : (s + 1) * n.chunk_pad]

    def pass_on(d, frm, into):
        return pltpu.make_async_remote_copy(
            src_ref=rs_out.at[frm],
            dst_ref=rs_in.at[into],
            send_sem=s3.at[d],
            recv_sem=r3.at[d],
            device_id=plane_device(peer(d)),
            device_id_type=MESH,
        )

    def start_pass(d, carry):
        pass_on(d, peer(d), me).start()
        return carry

    lax.fori_loop(1, n.plane, start_pass, 0)
    fin[...] = rs_out[me].astype(f32)

    def add_pass(d, carry):
        pass_on(d, peer(d), source(d)).wait_recv()
        fin[...] += rs_in[source(d)].astype(f32)
        return carry

    lax.fori_loop(1, n.plane, add_pass, 0)

    swap_back = pltpu.make_async_remote_copy(
        src_ref=fin.at[pl.ds(0, n.cols)],
        dst_ref=fin_in.at[pl.ds(0, n.cols)],
        send_sem=s4.at[0],
        recv_sem=r4.at[0],
        device_id=far,
        device_id_type=MESH,
    )

    def give_back(k):
        return pltpu.make_async_remote_copy(
            src_ref=fin.at[piece_rows(k)],
            dst_ref=fin_in.at[piece_rows(held_chunk)],
            send_sem=s4.at[1 + k],
            recv_sem=r4.at[1 + held_chunk],
            device_id=giver(k)[0],
            device_id_type=MESH,
        )

    def take_back(m):
        return pltpu.make_async_remote_copy(
            src_ref=fin.at[piece_rows(0)],
            dst_ref=fin_in.at[piece_rows(m)],
            send_sem=s4.at[1],
            recv_sem=r4.at[1 + m],
            device_id=target(m)[0],
            device_id_type=MESH,
        )

    @pl.when(crosses)
    def _():
        swap_back.start()

    @pl.when(jnp.logical_not(crosses))
    def _():
        fin_in[0 : n.cols] = fin[0 : n.cols]

    for k in range(n.quad):
        is_me = giver(k)[1]

        @pl.when(jnp.logical_not(is_me))
        def _():
            give_back(k).start()

        @pl.when(is_me)
        def _():
            fin_in[piece_rows(held_chunk)] = fin[piece_rows(k)]

    @pl.when(crosses)
    def _():
        swap_back.wait_recv()

    for m in range(n.chunks):

        @pl.when(jnp.logical_not(target(m)[1]))
        def _():
            take_back(m).wait_recv()

    for m in range(n.chunks):
        at = n.cols + m * n.chunk_pad
        c_pad[m * n.chunk : m * n.chunk + n.chunk_pad] = fin_in[at : at + n.chunk_pad]
    c_pad[0 : n.cols] = c_pad[0 : n.cols] + fin_in[0 : n.cols]
    out[...] = c_pad[...].T[0 : n.rows, 0 : n.cols]

    @pl.when(crosses)
    def _():
        swap.wait_send()
        swap_back.wait_send()

    for m in range(n.chunks):

        @pl.when(jnp.logical_not(target(m)[1]))
        def _():
            give(m).wait_send()

    for k in range(n.quad):

        @pl.when(jnp.logical_not(giver(k)[1]))
        def _():
            give_back(k).wait_send()

    def drain(d, carry):
        share(d, me).wait_send()
        pass_on(d, peer(d), me).wait_send()
        return carry

    lax.fori_loop(1, n.plane, drain, 0)


def per_device(mesh, coefficients, integrals, targets, orbital_pairs, phases):
    rows, cols = coefficients.shape
    n = plan_of(
        mesh, (rows * mesh.shape["tile"], cols * mesh.shape["wide"]), targets.shape, integrals.shape[0]
    )
    bf16, f32 = jnp.bfloat16, jnp.float32
    slot = (n.cols + n.quad * n.chunk_pad, LANES)
    total = n.own * LANES
    dma = pltpu.SemaphoreType.DMA
    vmem, anywhere = pl.BlockSpec(memory_space=pltpu.VMEM), pl.BlockSpec(memory_space=pl.ANY)
    return pl.pallas_call(
        functools.partial(kernel, n),
        out_shape=jax.ShapeDtypeStruct((n.rows, n.cols), f32),
        in_specs=[vmem, vmem, anywhere, anywhere, anywhere],
        out_specs=vmem,
        scratch_shapes=[
            pltpu.VMEM((3, n.exc, 2 * LANES), jnp.int32),
            pltpu.VMEM((3, LANES, 2 * LANES), jnp.int32),
            pltpu.VMEM((n.pair_pad, n.pair_pad), bf16),
            pltpu.VMEM((LANES, LANES), f32),
            pltpu.VMEM(slot, bf16),
            pltpu.VMEM(slot, bf16),
            pltpu.VMEM((n.plane, *slot), bf16),
            pltpu.VMEM((n.strings, LANES), f32),
            pltpu.VMEM((2 * LANES, n.strings), bf16),
            pltpu.VMEM((total, n.strings), bf16),
            pltpu.VMEM((n.own, LANES, LANES), bf16),
            pltpu.VMEM((2 * LANES, total), bf16),
            pltpu.VMEM((2 * LANES, n.strings), f32),
            pltpu.VMEM((n.plane, *slot), bf16),
            pltpu.VMEM((n.plane, *slot), bf16),
            pltpu.VMEM(slot, f32),
            pltpu.VMEM(slot, f32),
            dma((3,)),
            dma((1 + n.chunks,)),
            dma((1 + n.quad,)),
            dma((n.plane,)),
            dma((n.plane,)),
            dma((n.plane,)),
            dma((n.plane,)),
            dma((1 + n.quad,)),
            dma((1 + n.chunks,)),
        ],
        compiler_params=pltpu.CompilerParams(
            collective_id=0, has_side_effects=True, vmem_limit_bytes=56 * 1024 * 1024
        ),
        name="sigma",
    )(coefficients, integrals, targets, orbital_pairs, phases)


def solution(mesh):
    in_specs = (P("tile", "wide"), P(), P(), P(), P())
    return jax.shard_map(
        functools.partial(per_device, mesh),
        mesh=mesh,
        in_specs=in_specs,
        out_specs=P("tile", "wide"),
        check_vma=False,
    )
```

time: 653 us -> 85.9 us (0.13)
  waiting for transfers between devices: 322 us -> 0 us
  blocking collectives: 153 us -> 0 us
  Pallas kernels: 0 us -> 82.7 us
  other arithmetic: 66.1 us -> 0 us
  local copies, waits for them, and re-layouts: 45.9 us -> 2.89 us
  starting transfers between devices: 26.7 us -> 0 us
  matrix products: 25.1 us -> 0 us
  between operations: 13.5 us -> 0.01 us
    reduce_scatter x1 -> x0, waiting for transfers between devices: 302 us -> none  [per_device(): lax.psum_scatter(partial_value, 'wide', scatter_dimension=1, tiled=True)]
    all_gather x1 -> x0, blocking collectives: 153 us -> none  [per_device(): row_block = lax.all_gather(coefficients, 'wide', axis=1, tiled=True)]
    pallas_call x0 -> x1, Pallas kernels: none -> 82.7 us  [per_device(): pl.pallas_call(functools.partial(kernel, n), out_shape=jax.ShapeDtypeStru...]
    scatter-add x2 -> x0, other arithmetic: 62.4 us -> none  [the longest x1 31.2 us: per_device(): partial_value = jnp.zeros((row_count, total_cols), jnp.float32).at[:, fla...]
    gather x6 -> x0, local copies, waits for them, and re-layouts: 31.8 us -> none  [the longest x3 15.9 us: per_device(): values = row_block[:, own_targets] * own_sign[None]]
    all_to_all x2 -> x0, starting transfers between devices: 26.7 us -> none  [the longest x1 19.6 us: per_device(): lax.all_to_all(row_block, 'tile', split_axis=1, concat_axis=0, tiled=True)]
    dot_general x4 -> x0, matrix products: 25.1 us -> none  [the longest x2 14.2 us: couple(): jnp.einsum('abq,pq->abp', spread, integrals, preferred_element_type=jnp.f...]
    all_to_all x2 -> x0, waiting for transfers between devices: 20.2 us -> none  [the longest x1 17.4 us: per_device(): lax.all_to_all(flipped, 'tile', split_axis=0, concat_axis=1, tiled=True)]
  transfers between devices with their start and end apart: 3 -> 0, of which waited for: 3 -> 0; matrix products, arithmetic and copies ran while one was open for 6% -> 0% of each run, Pallas kernels for 0% -> 0%
where the time goes in v1:
time: 85.9 us; the launch traced here: 85.6 us
  Pallas kernels  82.7 us (96%)
  local copies, waits for them, and re-layouts  2.89 us (3%)
    pallas_call x1, Pallas kernels, per_device(): pl.pallas_call(functools.partial(kernel, n), out_shape=jax.ShapeDtypeStru...  82.7 us

profile of v1, /device:TPU:1, one launch (start us, length us, event | category | flops | bytes accessed | tf_op | source)
XLA Modules:
  0.0 85.6 jit_solution(6226459689986931234)
XLA Ops:
  0.0 1.4 %copy.6.coef = bf16[96,48]{1,0:T(8,128)(2,1)} copy(bf16[96,48]{0,1:T(8,128)(2,1)} %param.5) | data formatting | bytes 18432 | tf_op args[0]
  1.4 82.7 %sigma.1 = f32[96,48]{1,0:T(8,128)} custom-call(bf16[96,48]{1,0:T(8,128)(2,1)} %copy.6.coef, bf16[400,400]{1,0:T(8,128)(2,1)} %integ.1, s32[110,1536]{1,0:T(8,128)} %tgt.1, s32[110,1536]{1,0:T(8,128)} %prs.1, s32[110,1536]{1,0:T(8,128)} %phs.1), custom_call_target="tpu_custom_call" | custom-call | tf_op jit(solution)/shard_map/sigma/pallas_call | solution.py:488
  84.1 1.5 %copy.7 = f32[96,48]{0,1:T(8,128)} copy(f32[96,48]{1,0:T(8,128)} %sigma.1) | data formatting | bytes 36864 | tf_op jit(solution)/shard_map/sigma/pallas_call | solution.py:488

commit v2 on v1

v2 whole, which is shorter than its diff:
```python
import functools
import types

import jax
import jax.numpy as jnp
from jax import lax
from jax.experimental import pallas as pl
from jax.experimental.pallas import tpu as pltpu
from jax.sharding import PartitionSpec as P

LANES = 128
MESH = pl.DeviceIdType.MESH


def plan_of(mesh, coef_shape, exc_shape, pair_count):
    tiles, wides = mesh.shape["tile"], mesh.shape["wide"]
    xs = 4 if wides == 32 else 2
    ys = wides // (2 * xs)
    strings = coef_shape[0]
    rows, cols = strings // tiles, strings // wides
    spots = xs * ys
    halves = 2 if ys % 2 == 0 else 1
    chunks = tiles // 4
    chunk = cols // chunks
    return types.SimpleNamespace(
        tiles=tiles,
        wides=wides,
        xs=xs,
        ys=ys,
        plane=2 * spots,
        spots=spots,
        halves=halves,
        width=strings // halves,
        slot=cols + (tiles // 4) * (-(-chunk // 16) * 16),
        strings=strings,
        rows=rows,
        cols=cols,
        quad=tiles // 4,
        chunks=chunks,
        chunk=chunk,
        chunk_pad=-(-chunk // 16) * 16,
        sets=xs * ys // 2,
        own=strings // (xs * ys * 2),
        exc=exc_shape[0],
        pairs=pair_count,
        pair_pad=-(-pair_count // LANES) * LANES,
        step=8,
    )


def kernel(n, coef, integ, tgt, prs, phs, out, raw, tabs, g_pad, p_part, c_pad, first, hold, gath, xt, x_all,
           t_all, w_all, u_all, part, xa, sb, rb, sa, ra, ob, oa, in_b, in_a, fin, fin_in,
           s_tab, s1, r1, s2, r2, s5, r5, s6, r6, s3b, r3b, s3a, r3a, s4, r4):
    bf16, f32 = jnp.bfloat16, jnp.float32
    tile, wide = lax.axis_index("tile"), lax.axis_index("wide")
    core, zl = lax.rem(tile, 2), tile // 2
    x, zh, y = lax.rem(wide, n.xs), lax.rem(wide // n.xs, 2), wide // (2 * n.xs)
    spot = y * n.xs + x
    x_low, zl_odd = lax.rem(x, 2), lax.rem(zl, 2)

    def device(xx, yy, zzh, zzl, cc):
        return (zzl * 2 + cc, (yy * 2 + zzh) * n.xs + xx)

    def at_spot(j):
        return device(lax.rem(j, n.xs), j // n.xs, zh, zl, core)

    def other(d):
        return lax.rem(spot + d, n.spots)

    def flip(a, b):
        return lax.rem(a + b, 2)

    partner = device(x, y, zh, zl, 1 - core)
    crosses = zh != core
    far = device(x, y, 1 - zh, zl, 1 - core)
    my_quad, my_slot = tile // n.quad, lax.rem(tile, n.quad)
    to_x = (x // 2) * 2 + flip(x_low, my_quad // 2)
    to_core = lax.rem(my_quad, 2)

    def target(m):
        zz = 2 * m + x_low
        is_me = (to_x == x) & (to_core == core) & (zz == zl)
        return device(to_x, y, zh, zz, to_core), is_me

    from_x = (x // 2) * 2 + zl_odd
    held_quad = 2 * flip(x_low, zl_odd) + core
    held_set = y * (n.xs // 2) + x // 2

    def giver(k):
        t = held_quad * n.quad + k
        is_me = (from_x == x) & (t == tile)
        return device(from_x, y, zh, t // 2, lax.rem(t, 2)), is_me

    held_chunk = zl // 2

    barrier = pltpu.get_barrier_semaphore()

    def greet_one(whom):
        pl.semaphore_signal(barrier, inc=1, device_id=whom, device_id_type=MESH)

    def greet(d, carry):
        greet_one(at_spot(other(d)))
        return carry

    @pl.when(crosses)
    def _():
        greet_one(far)

    for m in range(n.chunks):
        where_to, is_me = target(m)

        @pl.when(jnp.logical_not(is_me))
        def _():
            greet_one(where_to)

    for k in range(n.quad):
        whose, is_me = giver(k)

        @pl.when(jnp.logical_not(is_me))
        def _():
            greet_one(whose)

    greet_one(partner)
    lax.fori_loop(1, n.spots, greet, 0)

    start = (spot * 2 + core) * n.own
    window = jnp.minimum(start // LANES * LANES, n.strings - 2 * LANES)
    window = pl.multiple_of(window, LANES)
    loads = [
        pltpu.make_async_copy(ref.at[:, pl.ds(window, 2 * LANES)], raw.at[i], s_tab.at[i])
        for i, ref in enumerate((tgt, prs, phs))
    ]
    for load in loads:
        load.start()

    c_pad[...] = jnp.zeros_like(c_pad)
    c_pad[0 : n.cols, 0 : n.rows] = coef[...].astype(f32)
    first[0 : n.cols] = c_pad[0 : n.cols].astype(bf16)
    for m in range(n.chunks):
        piece = c_pad[m * n.chunk : m * n.chunk + n.chunk_pad]
        at = n.cols + m * n.chunk_pad
        first[at : at + n.chunk_pad] = piece.astype(bf16)

    g_pad[...] = jnp.zeros_like(g_pad)
    g_pad[0 : n.pairs, 0 : n.pairs] = integ[...]
    tabs[...] = jnp.zeros_like(tabs)
    for load in loads:
        load.wait()
    tabs[:, 0 : n.exc] = raw[...]

    offset = start - window
    lane = lax.broadcasted_iota(jnp.int32, (LANES, LANES), 1).astype(f32).astype(bf16)
    one, zero = jnp.ones((), bf16), jnp.zeros((), bf16)

    def spread_col(col):
        return jnp.broadcast_to(col, (LANES, LANES)).astype(bf16)

    def build(it, carry):
        shift = lax.rem(2 * 2 * LANES - offset - it * n.step, 2 * LANES)
        t = pltpu.roll(tabs[0], shift, 1)[:, 0:LANES]
        q = pltpu.roll(tabs[1], shift, 1)[:, 0:LANES]
        s = pltpu.roll(tabs[2], shift, 1)[:, 0:LANES].astype(f32)
        t_hi, t_lo = (t // LANES).astype(f32), lax.rem(t, LANES).astype(f32)
        q_hi, q_lo = (q // LANES).astype(f32), lax.rem(q, LANES).astype(f32)
        for u in range(n.step):
            hi, lo = spread_col(q_hi[:, u : u + 1]), spread_col(q_lo[:, u : u + 1])
            sign = spread_col(s[:, u : u + 1])
            hot = jnp.where(lo == lane, sign, zero)
            for kt in range(n.pair_pad // LANES):
                p_part[u * LANES : (u + 1) * LANES, kt * LANES : (kt + 1) * LANES] = jnp.where(
                    hi == kt, hot, zero
                )
        picked = lax.dot_general(
            p_part[...], g_pad[...], (((1,), (1,)), ((), ())), preferred_element_type=f32
        ).astype(bf16)
        for u in range(n.step):
            b = it * n.step + u
            rows = pl.ds(pl.multiple_of(b * LANES, LANES), LANES)
            hi, lo = spread_col(t_hi[:, u : u + 1]), spread_col(t_lo[:, u : u + 1])
            hot = jnp.where(lo == lane, one, zero)
            for kt in range(n.strings // LANES):
                t_all[rows, kt * LANES : (kt + 1) * LANES] = jnp.where(hi == kt, hot, zero)
        for u in range(n.step):
            rows = slice(u * LANES, (u + 1) * LANES)
            w_all[it * n.step + u] = lax.dot_general(
                picked[rows], p_part[rows], (((1,), (1,)), ((), ())), preferred_element_type=f32
            ).astype(bf16)
        return carry

    builds = n.own // n.step
    cut_a, cut_b = max(1, builds // 6), max(1, builds * 2 // 3)
    lax.fori_loop(0, cut_a, build, 0)

    itself = jnp.int32(0)
    for m in range(n.chunks):
        itself = itself + target(m)[1].astype(jnp.int32)
    expected = n.spots + n.chunks + n.quad - 2 * itself + crosses.astype(jnp.int32)
    pl.semaphore_wait(barrier, expected)

    def piece_rows(k):
        return pl.ds(pl.multiple_of(n.cols + k * n.chunk_pad, 16), n.chunk_pad)

    swap = pltpu.make_async_remote_copy(
        src_ref=first.at[pl.ds(0, n.cols)],
        dst_ref=hold.at[pl.ds(0, n.cols)],
        send_sem=s1.at[0],
        recv_sem=r1.at[0],
        device_id=far,
        device_id_type=MESH,
    )

    def give(m):
        return pltpu.make_async_remote_copy(
            src_ref=first.at[piece_rows(m)],
            dst_ref=hold.at[piece_rows(my_slot)],
            send_sem=s1.at[1 + m],
            recv_sem=r1.at[1 + my_slot],
            device_id=target(m)[0],
            device_id_type=MESH,
        )

    def take(k):
        return pltpu.make_async_remote_copy(
            src_ref=first.at[piece_rows(0)],
            dst_ref=hold.at[piece_rows(k)],
            send_sem=s1.at[1],
            recv_sem=r1.at[1 + k],
            device_id=giver(k)[0],
            device_id_type=MESH,
        )

    @pl.when(crosses)
    def _():
        swap.start()

    @pl.when(jnp.logical_not(crosses))
    def _():
        hold[0 : n.cols] = first[0 : n.cols]

    for m in range(n.chunks):
        is_me = target(m)[1]

        @pl.when(jnp.logical_not(is_me))
        def _():
            give(m).start()

        @pl.when(is_me)
        def _():
            hold[piece_rows(my_slot)] = first[piece_rows(m)]

    lax.fori_loop(cut_a, cut_b, build, 0)

    @pl.when(crosses)
    def _():
        swap.wait_recv()

    for k in range(n.quad):

        @pl.when(jnp.logical_not(giver(k)[1]))
        def _():
            take(k).wait_recv()

    def share(to, frm):
        return pltpu.make_async_remote_copy(
            src_ref=hold,
            dst_ref=gath.at[core, frm],
            send_sem=s2.at[to],
            recv_sem=r2.at[frm],
            device_id=at_spot(to),
            device_id_type=MESH,
        )

    def relay(j, side):
        return pltpu.make_async_remote_copy(
            src_ref=gath.at[side, j],
            dst_ref=gath.at[side, j],
            send_sem=s5.at[j],
            recv_sem=r5.at[j],
            device_id=partner,
            device_id_type=MESH,
        )

    def start_share(d, carry):
        share(other(d), spot).start()
        return carry

    lax.fori_loop(1, n.spots, start_share, 0)
    gath[core, spot] = hold[...]
    relay(spot, core).start()

    lax.fori_loop(cut_b, builds, build, 0)

    def hand_on(d, carry):
        share(spot, other(d)).wait_recv()
        relay(other(d), core).start()
        return carry

    lax.fori_loop(1, n.spots, hand_on, 0)

    def wait_relay(j, carry):
        relay(j, 1 - core).wait_recv()
        return carry

    lax.fori_loop(0, n.spots, wait_relay, 0)

    for w in range(n.plane):
        yy, cc, xx = w // (2 * n.xs), w // n.xs % 2, w % n.xs
        xt[w * n.cols : (w + 1) * n.cols] = gath[cc, yy * n.xs + xx, 0 : n.cols].astype(f32)
    for kt in range(n.strings // LANES):
        at = slice(kt * LANES, (kt + 1) * LANES)
        x_all[0:LANES, at] = xt[at].T.astype(bf16)

    lane_i = lax.broadcasted_iota(jnp.int32, (LANES, LANES), 1)

    def alpha_piece(t):
        quad, slot = t // n.quad, t % n.quad
        at = n.cols + slot * n.chunk_pad
        pieces = []
        for s in range(n.sets):
            yy, xh = s // (n.xs // 2), s % (n.xs // 2)
            xx = 2 * xh + flip(zl_odd, quad // 2)
            pieces.append(gath[quad % 2, yy * n.xs + xx, at : at + n.chunk_pad].astype(f32))
        short = LANES - n.sets * n.chunk_pad
        if short:
            pieces.append(jnp.zeros((short, LANES), f32))
        return jnp.concatenate(pieces, axis=0)

    for four in range(n.tiles // 4):
        p0, p1, p2, p3 = (alpha_piece(4 * four + i) for i in range(4))
        p1, p2, p3 = pltpu.roll(p1, 96, 1), pltpu.roll(p2, 64, 1), pltpu.roll(p3, 32, 1)
        tiles3 = (
            jnp.where(lane_i < 96, p0, p1),
            jnp.where(lane_i < 64, p1, p2),
            jnp.where(lane_i < 32, p2, p3),
        )
        for i, value in enumerate(tiles3):
            at = (3 * four + i) * LANES
            x_all[LANES : 2 * LANES, at : at + LANES] = value.astype(bf16)

    many = min(8, n.own)

    def couple(it, carry):
        rows = pl.ds(pl.multiple_of(it * many * LANES, many * LANES), many * LANES)
        v = lax.dot_general(
            x_all[...], t_all[rows, :], (((1,), (1,)), ((), ())), preferred_element_type=f32
        ).astype(bf16)
        for u in range(many):
            value = jnp.dot(
                v[:, u * LANES : (u + 1) * LANES], w_all[it * many + u], preferred_element_type=f32
            )
            at = pl.ds(pl.multiple_of((it * many + u) * LANES, LANES), LANES)
            u_all[:, at] = value.astype(bf16)
        return carry

    lax.fori_loop(0, n.own // many, couple, 0)

    block = n.xs * n.cols

    def block_rows(yy, cc):
        return pl.ds(pl.multiple_of((yy * 2 + cc) * block, 16), block)

    def ys_of(h):
        return range(h * n.ys // n.halves, (h + 1) * n.ys // n.halves)

    def bases_of(h):
        return range(h * 4 // n.halves, (h + 1) * 4 // n.halves, 2)

    def cross_b(yy, cc):
        return pltpu.make_async_remote_copy(
            src_ref=sb.at[block_rows(yy, cc)],
            dst_ref=rb.at[block_rows(yy, cc)],
            send_sem=s6.at[yy],
            recv_sem=r6.at[yy],
            device_id=partner,
            device_id_type=MESH,
        )

    def cross_a(base, cc):
        return pltpu.make_async_remote_copy(
            src_ref=sa.at[base + cc],
            dst_ref=ra.at[base + cc],
            send_sem=s6.at[n.ys + base // 2],
            recv_sem=r6.at[n.ys + base // 2],
            device_id=partner,
            device_id_type=MESH,
        )

    def scatter(h):
        at = slice(h * n.width, (h + 1) * n.width)
        part[:, at] = jnp.dot(u_all[...], t_all[:, at], preferred_element_type=f32)

    def exchange(h):
        first_tile = h * n.width // LANES
        for kt in range(first_tile, first_tile + n.width // LANES):
            at = slice(kt * LANES, (kt + 1) * LANES)
            xt[at] = part[0:LANES, at].T
        for yy in ys_of(h):
            rows = block_rows(yy, 1 - core)
            sb[rows] = xt[rows].astype(bf16)
            cross_b(yy, 1 - core).start()
        per = n.tiles // 4 // n.halves
        for four in range(h * per, (h + 1) * per):
            t0, t1, t2 = (
                part[LANES : 2 * LANES, (3 * four + i) * LANES : (3 * four + i + 1) * LANES]
                for i in range(3)
            )
            roll = functools.partial(pltpu.roll, axis=1)
            values = (
                t0,
                jnp.where(lane_i < 32, roll(t0, 32), roll(t1, 32)),
                jnp.where(lane_i < 64, roll(t1, 64), roll(t2, 64)),
                roll(t2, 96),
            )
            for i, value in enumerate(values):
                t = 4 * four + i
                quad, slot = t // n.quad, t % n.quad
                for s in range(n.sets):
                    xa[quad, s, slot * n.chunk_pad : (slot + 1) * n.chunk_pad] = value[
                        s * n.chunk_pad : (s + 1) * n.chunk_pad
                    ]
        for base in bases_of(h):
            sa[base + 1 - core] = xa[base + 1 - core].astype(bf16)
            cross_a(base, 1 - core).start()

    def send_b(yy, xx):
        rows = pl.ds(pl.multiple_of(((yy * 2 + core) * n.xs + xx) * n.cols, 16), n.cols)
        to = yy * n.xs + xx
        return pltpu.make_async_remote_copy(
            src_ref=ob.at[rows],
            dst_ref=in_b.at[spot],
            send_sem=s3b.at[to],
            recv_sem=r3b.at[spot],
            device_id=at_spot(to),
            device_id_type=MESH,
        )

    def send_a(base, s):
        to = (s // (n.xs // 2)) * n.xs + 2 * lax.rem(s, n.xs // 2) + flip(zl_odd, base // 2)
        copy = pltpu.make_async_remote_copy(
            src_ref=oa.at[base + core, s],
            dst_ref=in_a.at[spot],
            send_sem=s3a.at[to],
            recv_sem=r3a.at[spot],
            device_id=at_spot(to),
            device_id_type=MESH,
        )
        return copy, to

    def spread_out(h):
        for yy in ys_of(h):
            rows = block_rows(yy, core)
            cross_b(yy, core).wait_recv()
            total = xt[rows] + rb[rows].astype(f32)
            xt[rows] = total
            ob[rows] = total.astype(bf16)
            for i in range(n.xs):
                xx = lax.rem(x + i, n.xs)

                @pl.when(jnp.logical_or(xx != x, y != yy))
                def _():
                    send_b(yy, xx).start()

        for base in bases_of(h):
            cross_a(base, core).wait_recv()
            total = xa[base + core] + ra[base + core].astype(f32)
            xa[base + core] = total
            oa[base + core] = total.astype(bf16)
            for i in range(n.sets):
                copy, to = send_a(base, lax.rem(held_set + i, n.sets))

                @pl.when(to != spot)
                def _():
                    copy.start()

    scatter(0)
    exchange(0)
    for h in range(1, n.halves):
        scatter(h)
        spread_out(h - 1)
        exchange(h)
    spread_out(n.halves - 1)

    mine = pl.ds(pl.multiple_of(((y * 2 + core) * n.xs + x) * n.cols, 16), n.cols)
    fin[0 : n.cols] = xt[mine]
    fin[n.cols :] = xa[held_quad, held_set]

    def add_in(d, carry):
        j = other(d)
        pltpu.make_async_remote_copy(
            src_ref=ob.at[pl.ds(0, n.cols)],
            dst_ref=in_b.at[j],
            send_sem=s3b.at[j],
            recv_sem=r3b.at[j],
            device_id=at_spot(j),
            device_id_type=MESH,
        ).wait_recv()
        fin[0 : n.cols] += in_b[j].astype(f32)
        pltpu.make_async_remote_copy(
            src_ref=oa.at[0, 0],
            dst_ref=in_a.at[j],
            send_sem=s3a.at[j],
            recv_sem=r3a.at[j],
            device_id=at_spot(j),
            device_id_type=MESH,
        ).wait_recv()
        fin[n.cols :] += in_a[j].astype(f32)
        return carry

    lax.fori_loop(1, n.spots, add_in, 0)

    swap_back = pltpu.make_async_remote_copy(
        src_ref=fin.at[pl.ds(0, n.cols)],
        dst_ref=fin_in.at[pl.ds(0, n.cols)],
        send_sem=s4.at[0],
        recv_sem=r4.at[0],
        device_id=far,
        device_id_type=MESH,
    )

    def give_back(k):
        return pltpu.make_async_remote_copy(
            src_ref=fin.at[piece_rows(k)],
            dst_ref=fin_in.at[piece_rows(held_chunk)],
            send_sem=s4.at[1 + k],
            recv_sem=r4.at[1 + held_chunk],
            device_id=giver(k)[0],
            device_id_type=MESH,
        )

    def take_back(m):
        return pltpu.make_async_remote_copy(
            src_ref=fin.at[piece_rows(0)],
            dst_ref=fin_in.at[piece_rows(m)],
            send_sem=s4.at[1],
            recv_sem=r4.at[1 + m],
            device_id=target(m)[0],
            device_id_type=MESH,
        )

    @pl.when(crosses)
    def _():
        swap_back.start()

    @pl.when(jnp.logical_not(crosses))
    def _():
        fin_in[0 : n.cols] = fin[0 : n.cols]

    for k in range(n.quad):
        is_me = giver(k)[1]

        @pl.when(jnp.logical_not(is_me))
        def _():
            give_back(k).start()

        @pl.when(is_me)
        def _():
            fin_in[piece_rows(held_chunk)] = fin[piece_rows(k)]

    @pl.when(crosses)
    def _():
        swap.wait_send()

    for m in range(n.chunks):

        @pl.when(jnp.logical_not(target(m)[1]))
        def _():
            give(m).wait_send()

    def drain(d, carry):
        j = other(d)
        share(j, spot).wait_send()
        send_b(j // n.xs, lax.rem(j, n.xs)).wait_send()
        pltpu.make_async_remote_copy(
            src_ref=oa.at[0, 0],
            dst_ref=in_a.at[j],
            send_sem=s3a.at[j],
            recv_sem=r3a.at[j],
            device_id=at_spot(j),
            device_id_type=MESH,
        ).wait_send()
        return carry

    lax.fori_loop(1, n.spots, drain, 0)

    def drain_relay(j, carry):
        relay(j, core).wait_send()
        return carry

    lax.fori_loop(0, n.spots, drain_relay, 0)
    for yy in range(n.ys):
        cross_b(yy, 1 - core).wait_send()
    for base in (0, 2):
        cross_a(base, 1 - core).wait_send()

    @pl.when(crosses)
    def _():
        swap_back.wait_recv()
        swap_back.wait_send()

    for m in range(n.chunks):

        @pl.when(jnp.logical_not(target(m)[1]))
        def _():
            take_back(m).wait_recv()

    for k in range(n.quad):

        @pl.when(jnp.logical_not(giver(k)[1]))
        def _():
            give_back(k).wait_send()

    for m in range(n.chunks):
        at = n.cols + m * n.chunk_pad
        c_pad[m * n.chunk : m * n.chunk + n.chunk_pad] = fin_in[at : at + n.chunk_pad]
    out[...] = c_pad[0 : n.cols, 0 : n.rows] + fin_in[0 : n.cols, 0 : n.rows]


def per_device(mesh, coefficients, integrals, targets, orbital_pairs, phases):
    rows, cols = coefficients.shape
    n = plan_of(
        mesh, (rows * mesh.shape["tile"], cols * mesh.shape["wide"]), targets.shape, integrals.shape[0]
    )
    bf16, f32 = jnp.bfloat16, jnp.float32
    total = n.own * LANES
    alpha = n.slot - n.cols
    dma = pltpu.SemaphoreType.DMA
    vmem, anywhere = pl.BlockSpec(memory_space=pltpu.VMEM), pl.BlockSpec(memory_space=pl.ANY)
    sigma_t = pl.pallas_call(
        functools.partial(kernel, n),
        out_shape=jax.ShapeDtypeStruct((n.cols, n.rows), f32),
        in_specs=[vmem, vmem, anywhere, anywhere, anywhere],
        out_specs=vmem,
        scratch_shapes=[
            pltpu.VMEM((3, n.exc, 2 * LANES), jnp.int32),
            pltpu.VMEM((3, LANES, 2 * LANES), jnp.int32),
            pltpu.VMEM((n.pair_pad, n.pair_pad), bf16),
            pltpu.VMEM((n.step * LANES, n.pair_pad), bf16),
            pltpu.VMEM((LANES, LANES), f32),
            pltpu.VMEM((n.slot, LANES), bf16),
            pltpu.VMEM((n.slot, LANES), bf16),
            pltpu.VMEM((2, n.spots, n.slot, LANES), bf16),
            pltpu.VMEM((n.strings, LANES), f32),
            pltpu.VMEM((2 * LANES, n.strings), bf16),
            pltpu.VMEM((total, n.strings), bf16),
            pltpu.VMEM((n.own, LANES, LANES), bf16),
            pltpu.VMEM((2 * LANES, total), bf16),
            pltpu.VMEM((2 * LANES, n.strings), f32),
            pltpu.VMEM((4, n.sets, alpha, LANES), f32),
            pltpu.VMEM((n.strings, LANES), bf16),
            pltpu.VMEM((n.strings, LANES), bf16),
            pltpu.VMEM((4, n.sets, alpha, LANES), bf16),
            pltpu.VMEM((4, n.sets, alpha, LANES), bf16),
            pltpu.VMEM((n.strings, LANES), bf16),
            pltpu.VMEM((4, n.sets, alpha, LANES), bf16),
            pltpu.VMEM((n.spots, n.cols, LANES), bf16),
            pltpu.VMEM((n.spots, alpha, LANES), bf16),
            pltpu.VMEM((n.slot, LANES), f32),
            pltpu.VMEM((n.slot, LANES), f32),
            dma((3,)),
            dma((1 + n.chunks,)),
            dma((1 + n.quad,)),
            dma((n.spots,)),
            dma((n.spots,)),
            dma((n.spots,)),
            dma((n.spots,)),
            dma((n.ys + 2,)),
            dma((n.ys + 2,)),
            dma((n.spots,)),
            dma((n.spots,)),
            dma((n.spots,)),
            dma((n.spots,)),
            dma((1 + n.quad,)),
            dma((1 + n.chunks,)),
        ],
        compiler_params=pltpu.CompilerParams(
            collective_id=0, has_side_effects=True, vmem_limit_bytes=56 * 1024 * 1024
        ),
        name="sigma",
    )(coefficients.T, integrals, targets, orbital_pairs, phases)
    return sigma_t.T


def solution(mesh):
    in_specs = (P("tile", "wide"), P(), P(), P(), P())
    return jax.shard_map(
        functools.partial(per_device, mesh),
        mesh=mesh,
        in_specs=in_specs,
        out_specs=P("tile", "wide"),
        check_vma=False,
    )
```

time: 85.9 us -> 65.2 us (0.76)
  Pallas kernels: 82.7 us -> 63.6 us
  local copies, waits for them, and re-layouts: 2.89 us -> 1.35 us
    pallas_call x1, Pallas kernels: 82.7 us -> 63.6 us  [per_device(): pl.pallas_call(functools.partial(kernel, n), out_shape=jax.ShapeDtypeStru...]
    pallas_call x1 -> x0, local copies, waits for them, and re-layouts: 1.49 us -> none  [per_device(): pl.pallas_call(functools.partial(kernel, n), out_shape=jax.ShapeDtypeStru...]
where the time goes in v2:
time: 65.2 us; the launch traced here: 65 us
  Pallas kernels  63.6 us (98%)
  local copies, waits for them, and re-layouts  1.35 us (2%)
    pallas_call x1, Pallas kernels, per_device(): pl.pallas_call(functools.partial(kernel, n), out_shape=jax.ShapeDtypeStru...  63.6 us
    unnamed x1, local copies, waits for them, and re-layouts  1.35 us

profile of v2, /device:TPU:1, one launch (start us, length us, event | category | flops | bytes accessed | tf_op | source)
XLA Modules:
  0.0 65.0 jit_solution(16913123276337991200)
XLA Ops:
  0.0 63.6 %sigma.1 = f32[48,96]{1,0:T(8,128)} custom-call(bf16[48,96]{1,0:T(8,128)(2,1)} %bitcast.3, bf16[400,400]{1,0:T(8,128)(2,1)} %integ.1, s32[110,1536]{1,0:T(8,128)} %tgt.1, s32[110,1536]{1,0:T(8,128)} %prs.1, s32[110,1536]{1,0:T(8,128)} %phs.1), custom_call_target="tpu_custom_call" | custom-call | tf_op jit(solution)/shard_map/sigma/pallas_call | solution.py:628
  63.6 1.3 %copy.7 = f32[96,48]{0,1:T(8,128)} copy(f32[96,48]{0,1:T(8,128)} %bitcast.2) | data formatting | bytes 36864

commit v3 on v0

v3 whole, which is shorter than its diff:
```python
import functools
import types

import jax
import jax.numpy as jnp
from jax import lax
from jax.experimental import pallas as pl
from jax.experimental.pallas import tpu as pltpu
from jax.sharding import PartitionSpec as P

LANES = 128
MESH = pl.DeviceIdType.MESH


def plan_of(mesh, coef_shape, exc_shape, pair_count):
    tiles, wides = mesh.shape["tile"], mesh.shape["wide"]
    xs = 4 if wides == 32 else 2
    ys = wides // (2 * xs)
    zs = tiles // 2
    strings = coef_shape[0]
    ranges = strings // (3 * LANES)
    return types.SimpleNamespace(
        tiles=tiles,
        xs=xs,
        ys=ys,
        zs=zs,
        spots=xs * ys,
        strings=strings,
        rows=strings // tiles,
        cols=strings // wides,
        own=strings // (xs * ys * 2),
        exc=exc_shape[0],
        pairs=pair_count,
        pair_pad=-(-pair_count // LANES) * LANES,
        step=8,
        ranges=ranges,
        order=sorted(range(ranges), key=lambda h: -abs(2 * h - ranges + 1)),
        width=strings // ranges,
    )


def kernel(n, coef, integ, tgt, prs, phs, out, raw, tabs, g_pad, p_part, c_pad, first, hold, gath_b, gath_a,
           xt, x_all, t_all, w_all, u_all, part, xa, sb, rb, ob, sa, ra, sx, rx, oa, in_b, in_a, fin, fin_in,
           s_tab, s1, r1, s2b, r2b, s5b, r5b, s2a, r2a, sxa, rxa, s5a, r5a, s6b, r6b, s6a, r6a,
           s3b, r3b, s7, r7, s8, r8, s4, r4):
    bf16, f32 = jnp.bfloat16, jnp.float32
    tile, wide = lax.axis_index("tile"), lax.axis_index("wide")
    core, zl = lax.rem(tile, 2), tile // 2
    x, zh, y = lax.rem(wide, n.xs), lax.rem(wide // n.xs, 2), wide // (2 * n.xs)
    spot = y * n.xs + x
    x_low, x_high = lax.rem(x, 2), x // 2

    def device(xx, yy, zzh, zzl, cc):
        return (zzl * 2 + cc, (yy * 2 + zzh) * n.xs + xx)

    def at_spot(j):
        return device(lax.rem(j, n.xs), j // n.xs, zh, zl, core)

    def on_line(z):
        return device(x, y, zh, z, core)

    def other(d):
        return lax.rem(spot + d, n.spots)

    def other_z(d):
        return lax.rem(zl + d, n.zs)

    partner = device(x, y, zh, zl, 1 - core)
    mate = device(x_high * 2 + 1 - x_low, y, zh, zl, core)
    half = n.zs // 2
    far_z = lax.rem(zl + half + n.zs * core, 2 * n.zs)
    far_out = device(x, y, far_z // n.zs, lax.rem(far_z, n.zs), zh)
    back_z = zh * n.zs + zl + 2 * n.zs - half
    back_zl = lax.rem(back_z, n.zs)
    far_in = device(x, y, core, back_zl, lax.rem(back_z - back_zl, 2 * n.zs) // n.zs)

    def remote(src, dst, send, recv, to):
        return pltpu.make_async_remote_copy(
            src_ref=src, dst_ref=dst, send_sem=send, recv_sem=recv, device_id=to, device_id_type=MESH
        )

    place = lax.rem(y * (n.xs // 2) + x_high + zl, n.zs)
    start = ((x_low * 2 + core) * n.zs + place) * n.own
    window = jnp.minimum(start // LANES * LANES, n.strings - 2 * LANES)
    window = pl.multiple_of(window, LANES)
    loads = [
        pltpu.make_async_copy(ref.at[:, pl.ds(window, 2 * LANES)], raw.at[i], s_tab.at[i])
        for i, ref in enumerate((tgt, prs, phs))
    ]
    for load in loads:
        load.start()

    barrier = pltpu.get_barrier_semaphore()

    def greet(whom):
        pl.semaphore_signal(barrier, inc=1, device_id=whom, device_id_type=MESH)

    def greet_line(d, carry):
        greet(on_line(other_z(d)))
        return carry

    def greet_plane(d, carry):
        greet(at_spot(other(d)))
        return carry

    greet(far_out)
    greet(far_in)
    lax.fori_loop(1, n.zs, greet_line, 0)
    lax.fori_loop(1, n.spots, greet_plane, 0)
    greet(partner)

    c_pad[...] = jnp.zeros_like(c_pad)
    c_pad[:, 0 : n.rows] = coef[...].astype(f32)
    first[...] = c_pad[...].astype(bf16)

    g_pad[...] = jnp.zeros_like(g_pad)
    g_pad[0 : n.pairs, 0 : n.pairs] = integ[...]
    tabs[...] = jnp.zeros_like(tabs)
    for load in loads:
        load.wait()
    tabs[:, 0 : n.exc] = raw[...]

    offset = start - window
    lane = lax.broadcasted_iota(jnp.int32, (LANES, LANES), 1).astype(f32).astype(bf16)
    one, zero = jnp.ones((), bf16), jnp.zeros((), bf16)

    def spread_col(col):
        return jnp.broadcast_to(col, (LANES, LANES)).astype(bf16)

    def build(it, carry):
        shift = lax.rem(2 * 2 * LANES - offset - it * n.step, 2 * LANES)
        t = pltpu.roll(tabs[0], shift, 1)[:, 0:LANES]
        q = pltpu.roll(tabs[1], shift, 1)[:, 0:LANES]
        s = pltpu.roll(tabs[2], shift, 1)[:, 0:LANES].astype(f32)
        t_hi, t_lo = (t // LANES).astype(f32), lax.rem(t, LANES).astype(f32)
        q_hi, q_lo = (q // LANES).astype(f32), lax.rem(q, LANES).astype(f32)
        for u in range(n.step):
            hi, lo = spread_col(q_hi[:, u : u + 1]), spread_col(q_lo[:, u : u + 1])
            sign = spread_col(s[:, u : u + 1])
            hot = jnp.where(lo == lane, sign, zero)
            for kt in range(n.pair_pad // LANES):
                p_part[u * LANES : (u + 1) * LANES, kt * LANES : (kt + 1) * LANES] = jnp.where(
                    hi == kt, hot, zero
                )
        picked = lax.dot_general(
            p_part[...], g_pad[...], (((1,), (1,)), ((), ())), preferred_element_type=f32
        ).astype(bf16)
        for u in range(n.step):
            b = it * n.step + u
            rows = pl.ds(pl.multiple_of(b * LANES, LANES), LANES)
            hi, lo = spread_col(t_hi[:, u : u + 1]), spread_col(t_lo[:, u : u + 1])
            hot = jnp.where(lo == lane, one, zero)
            for kt in range(n.strings // LANES):
                t_all[rows, kt * LANES : (kt + 1) * LANES] = jnp.where(hi == kt, hot, zero)
        for u in range(n.step):
            rows = slice(u * LANES, (u + 1) * LANES)
            w_all[it * n.step + u] = lax.dot_general(
                picked[rows], p_part[rows], (((1,), (1,)), ((), ())), preferred_element_type=f32
            ).astype(bf16)
        return carry

    builds = n.own // n.step
    cut_a, cut_b = max(1, builds // 3), max(1, builds * 5 // 6)
    lax.fori_loop(0, cut_a, build, 0)

    pl.semaphore_wait(barrier, 2 + n.zs - 1 + n.spots - 1 + 1)

    def line(to, frm):
        return remote(first, gath_a.at[core, x_low, frm], s2a.at[to], r2a.at[frm], on_line(to))

    def to_mate(z, side):
        ref = gath_a.at[core, side, z]
        return remote(ref, ref, sxa.at[z], rxa.at[z], mate)

    def relay_a(z, side, cc):
        ref = gath_a.at[cc, side, z]
        return remote(ref, ref, s5a.at[side, z], r5a.at[side, z], partner)

    def share(to, frm):
        return remote(hold, gath_b.at[core, frm], s2b.at[to], r2b.at[frm], at_spot(to))

    def relay_b(j, cc):
        ref = gath_b.at[cc, j]
        return remote(ref, ref, s5b.at[j], r5b.at[j], partner)

    forth = remote(first, hold, s1.at[0], r1.at[0], far_out)
    forth.start()

    def start_line(d, carry):
        line(other_z(d), zl).start()
        return carry

    lax.fori_loop(1, n.zs, start_line, 0)
    gath_a[core, x_low, zl] = first[...]
    to_mate(zl, x_low).start()
    relay_a(zl, x_low, core).start()

    lax.fori_loop(cut_a, cut_b, build, 0)

    forth.wait_recv()

    def start_share(d, carry):
        share(other(d), spot).start()
        return carry

    lax.fori_loop(1, n.spots, start_share, 0)
    gath_b[core, spot] = hold[...]
    relay_b(spot, core).start()

    lax.fori_loop(cut_b, builds, build, 0)

    def hand_line(d, carry):
        z = other_z(d)
        line(zl, z).wait_recv()
        to_mate(z, x_low).start()
        relay_a(z, x_low, core).start()
        return carry

    lax.fori_loop(1, n.zs, hand_line, 0)

    def hand_plane(d, carry):
        j = other(d)
        share(spot, j).wait_recv()
        relay_b(j, core).start()
        return carry

    lax.fori_loop(1, n.spots, hand_plane, 0)

    def hand_mate(d, carry):
        z = other_z(d)
        to_mate(z, 1 - x_low).wait_recv()
        relay_a(z, 1 - x_low, core).start()
        return carry

    lax.fori_loop(0, n.zs, hand_mate, 0)

    def wait_relay_b(j, carry):
        relay_b(j, 1 - core).wait_recv()
        return carry

    lax.fori_loop(0, n.spots, wait_relay_b, 0)

    for w in range(2 * n.spots):
        yy, cc, xx = w // (2 * n.xs), w // n.xs % 2, w % n.xs
        xt[w * n.cols : (w + 1) * n.cols] = gath_b[cc, yy * n.xs + xx].astype(f32)
    for kt in range(n.strings // LANES):
        at = slice(kt * LANES, (kt + 1) * LANES)
        x_all[0:LANES, at] = xt[at].T.astype(bf16)

    def wait_relay_a(z, carry):
        relay_a(z, 0, 1 - core).wait_recv()
        relay_a(z, 1, 1 - core).wait_recv()
        return carry

    lax.fori_loop(0, n.zs, wait_relay_a, 0)

    lane_i = lax.broadcasted_iota(jnp.int32, (LANES, LANES), 1)
    spare = jnp.zeros((LANES - 2 * n.cols, LANES), f32)

    def alpha_piece(t):
        low, high = (gath_a[t % 2, side, t // 2].astype(f32) for side in range(2))
        return jnp.concatenate([low, high, spare], axis=0)

    for four in range(n.tiles // 4):
        p0, p1, p2, p3 = (alpha_piece(4 * four + i) for i in range(4))
        p1, p2, p3 = pltpu.roll(p1, 96, 1), pltpu.roll(p2, 64, 1), pltpu.roll(p3, 32, 1)
        tiles3 = (
            jnp.where(lane_i < 96, p0, p1),
            jnp.where(lane_i < 64, p1, p2),
            jnp.where(lane_i < 32, p2, p3),
        )
        for i, value in enumerate(tiles3):
            at = (3 * four + i) * LANES
            x_all[LANES : 2 * LANES, at : at + LANES] = value.astype(bf16)

    many = min(8, n.own)

    def couple(it, carry):
        rows = pl.ds(pl.multiple_of(it * many * LANES, many * LANES), many * LANES)
        v = lax.dot_general(
            x_all[...], t_all[rows, :], (((1,), (1,)), ((), ())), preferred_element_type=f32
        ).astype(bf16)
        for u in range(many):
            value = jnp.dot(
                v[:, u * LANES : (u + 1) * LANES], w_all[it * many + u], preferred_element_type=f32
            )
            at = pl.ds(pl.multiple_of((it * many + u) * LANES, LANES), LANES)
            u_all[:, at] = value.astype(bf16)
        return carry

    lax.fori_loop(0, n.own // many, couple, 0)

    block = n.xs * n.cols
    keep = pl.ds(pl.multiple_of(x_low * n.cols, 16), n.cols)
    pass_on = pl.ds(pl.multiple_of((1 - x_low) * n.cols, 16), n.cols)

    def block_rows(yy, cc):
        return pl.ds(pl.multiple_of((yy * 2 + cc) * block, 16), block)

    def ys_of(h):
        return range(h * n.ys // n.ranges, (h + 1) * n.ys // n.ranges)

    def zs_of(h):
        return range(h * n.zs // n.ranges, (h + 1) * n.zs // n.ranges)

    def cross_b(yy, cc):
        rows = block_rows(yy, cc)
        return remote(sb.at[rows], rb.at[rows], s6b.at[yy], r6b.at[yy], partner)

    def cross_a(z, cc):
        return remote(sa.at[2 * z + cc], ra.at[2 * z + cc], s6a.at[z], r6a.at[z], partner)

    def across(z):
        return remote(sx.at[z], rx.at[z], s7.at[z], r7.at[z], mate)

    def down_line(to, frm):
        return remote(oa.at[to], in_a.at[frm], s8.at[to], r8.at[frm], on_line(to))

    def to_plane(rows, to, frm):
        return remote(ob.at[rows], in_b.at[frm], s3b.at[to], r3b.at[frm], at_spot(to))

    def scatter(h):
        at = slice(h * n.width, (h + 1) * n.width)
        part[:, at] = jnp.dot(u_all[...], t_all[:, at], preferred_element_type=f32)

    def sum_cores(h):
        t0, t1, t2 = (
            part[LANES : 2 * LANES, (3 * h + i) * LANES : (3 * h + i + 1) * LANES] for i in range(3)
        )
        roll = functools.partial(pltpu.roll, axis=1)
        values = (
            t0,
            jnp.where(lane_i < 32, roll(t0, 32), roll(t1, 32)),
            jnp.where(lane_i < 64, roll(t1, 64), roll(t2, 64)),
            roll(t2, 96),
        )
        for i, value in enumerate(values):
            xa[4 * h + i] = value[0 : 2 * n.cols]
        for z in zs_of(h):
            sa[2 * z + 1 - core] = xa[2 * z + 1 - core].astype(bf16)
            cross_a(z, 1 - core).start()
        for kt in range(3 * h, 3 * h + 3):
            at = slice(kt * LANES, (kt + 1) * LANES)
            xt[at] = part[0:LANES, at].T
        for yy in ys_of(h):
            rows = block_rows(yy, 1 - core)
            sb[rows] = xt[rows].astype(bf16)
            cross_b(yy, 1 - core).start()

    def sum_mates(h):
        for z in zs_of(h):
            cross_a(z, core).wait_recv()
            xa[2 * z + core] = xa[2 * z + core] + ra[2 * z + core].astype(f32)
            sx[z] = xa[2 * z + core, pass_on].astype(bf16)
            across(z).start()
        for yy in ys_of(h):
            rows = block_rows(yy, core)
            cross_b(yy, core).wait_recv()
            total = xt[rows] + rb[rows].astype(f32)
            xt[rows] = total
            ob[rows] = total.astype(bf16)
            for i in range(n.xs):
                xx = lax.rem(x + i, n.xs)
                rows = pl.ds(pl.multiple_of(((yy * 2 + core) * n.xs + xx) * n.cols, 16), n.cols)

                @pl.when(jnp.logical_or(xx != x, y != yy))
                def _():
                    to_plane(rows, yy * n.xs + xx, spot).start()

    def sum_line(h):
        for z in zs_of(h):
            across(z).wait_recv()
            total = xa[2 * z + core, keep] + rx[z].astype(f32)
            xa[2 * z + core, keep] = total
            oa[z] = total.astype(bf16)

            @pl.when(z != zl)
            def _():
                down_line(z, zl).start()

    for i in range(n.ranges + 2):
        if i < n.ranges:
            scatter(n.order[i])
        if 0 <= i - 2 < n.ranges:
            sum_line(n.order[i - 2])
        if 0 <= i - 1 < n.ranges:
            sum_mates(n.order[i - 1])
        if i < n.ranges:
            sum_cores(n.order[i])

    mine = pl.ds(pl.multiple_of(((y * 2 + core) * n.xs + x) * n.cols, 16), n.cols)
    fin[...] = xt[mine]

    def add_plane(d, carry):
        j = other(d)
        to_plane(pl.ds(0, n.cols), spot, j).wait_recv()
        fin[...] += in_b[j].astype(f32)
        return carry

    lax.fori_loop(1, n.spots, add_plane, 0)
    back = remote(fin, fin_in, s4.at[0], r4.at[0], far_in)
    back.start()

    c_pad[...] = xa[2 * zl + core, keep]

    def add_line(d, carry):
        z = other_z(d)
        down_line(zl, z).wait_recv()
        c_pad[...] += in_a[z].astype(f32)
        return carry

    lax.fori_loop(1, n.zs, add_line, 0)

    forth.wait_send()

    def drain_line(d, carry):
        z = other_z(d)
        line(z, zl).wait_send()
        down_line(z, zl).wait_send()
        return carry

    lax.fori_loop(1, n.zs, drain_line, 0)

    def drain_line_all(z, carry):
        to_mate(z, x_low).wait_send()
        relay_a(z, 0, core).wait_send()
        relay_a(z, 1, core).wait_send()
        cross_a(z, 1 - core).wait_send()
        across(z).wait_send()
        return carry

    lax.fori_loop(0, n.zs, drain_line_all, 0)

    def drain_plane(d, carry):
        j = other(d)
        share(j, spot).wait_send()
        to_plane(pl.ds(0, n.cols), j, spot).wait_send()
        return carry

    lax.fori_loop(1, n.spots, drain_plane, 0)

    def drain_plane_all(j, carry):
        relay_b(j, core).wait_send()
        return carry

    lax.fori_loop(0, n.spots, drain_plane_all, 0)
    for yy in range(n.ys):
        cross_b(yy, 1 - core).wait_send()

    back.wait_recv()
    out[...] = c_pad[:, 0 : n.rows] + fin_in[:, 0 : n.rows]
    back.wait_send()


def per_device(mesh, coefficients, integrals, targets, orbital_pairs, phases):
    rows, cols = coefficients.shape
    n = plan_of(
        mesh, (rows * mesh.shape["tile"], cols * mesh.shape["wide"]), targets.shape, integrals.shape[0]
    )
    bf16, f32 = jnp.bfloat16, jnp.float32
    total = n.own * LANES
    piece = (n.cols, LANES)
    dma, vmem = pltpu.SemaphoreType.DMA, pltpu.VMEM
    here, anywhere = pl.BlockSpec(memory_space=pltpu.VMEM), pl.BlockSpec(memory_space=pl.ANY)
    sigma_t = pl.pallas_call(
        functools.partial(kernel, n),
        out_shape=jax.ShapeDtypeStruct((n.cols, n.rows), f32),
        in_specs=[here, here, anywhere, anywhere, anywhere],
        out_specs=here,
        scratch_shapes=[
            vmem((3, n.exc, 2 * LANES), jnp.int32),
            vmem((3, LANES, 2 * LANES), jnp.int32),
            vmem((n.pair_pad, n.pair_pad), bf16),
            vmem((n.step * LANES, n.pair_pad), bf16),
            vmem(piece, f32),
            vmem(piece, bf16),
            vmem(piece, bf16),
            vmem((2, n.spots, *piece), bf16),
            vmem((2, 2, n.zs, *piece), bf16),
            vmem((n.strings, LANES), f32),
            vmem((2 * LANES, n.strings), bf16),
            vmem((total, n.strings), bf16),
            vmem((n.own, LANES, LANES), bf16),
            vmem((2 * LANES, total), bf16),
            vmem((2 * LANES, n.strings), f32),
            vmem((n.tiles, 2 * n.cols, LANES), f32),
            vmem((n.strings, LANES), bf16),
            vmem((n.strings, LANES), bf16),
            vmem((n.strings, LANES), bf16),
            vmem((n.tiles, 2 * n.cols, LANES), bf16),
            vmem((n.tiles, 2 * n.cols, LANES), bf16),
            vmem((n.zs, *piece), bf16),
            vmem((n.zs, *piece), bf16),
            vmem((n.zs, *piece), bf16),
            vmem((n.spots, *piece), bf16),
            vmem((n.zs, *piece), bf16),
            vmem(piece, f32),
            vmem(piece, f32),
            dma((3,)),
            dma((1,)),
            dma((1,)),
            dma((n.spots,)),
            dma((n.spots,)),
            dma((n.spots,)),
            dma((n.spots,)),
            dma((n.zs,)),
            dma((n.zs,)),
            dma((n.zs,)),
            dma((n.zs,)),
            dma((2, n.zs)),
            dma((2, n.zs)),
            dma((n.ys,)),
            dma((n.ys,)),
            dma((n.zs,)),
            dma((n.zs,)),
            dma((n.spots,)),
            dma((n.spots,)),
            dma((n.zs,)),
            dma((n.zs,)),
            dma((n.zs,)),
            dma((n.zs,)),
            dma((1,)),
            dma((1,)),
        ],
        compiler_params=pltpu.CompilerParams(
            collective_id=0, has_side_effects=True, vmem_limit_bytes=56 * 1024 * 1024
        ),
        name="sigma",
    )(coefficients.T, integrals, targets, orbital_pairs, phases)
    return sigma_t.T


def solution(mesh):
    in_specs = (P("tile", "wide"), P(), P(), P(), P())
    return jax.shard_map(
        functools.partial(per_device, mesh),
        mesh=mesh,
        in_specs=in_specs,
        out_specs=P("tile", "wide"),
        check_vma=False,
    )
```

time: 653 us -> 60.7 us (0.09)
  waiting for transfers between devices: 322 us -> 0 us
  blocking collectives: 153 us -> 0 us
  other arithmetic: 66.1 us -> 0 us
  Pallas kernels: 0 us -> 59.1 us
  local copies, waits for them, and re-layouts: 45.9 us -> 1.35 us
  starting transfers between devices: 26.7 us -> 0 us
  matrix products: 25.1 us -> 0 us
  between operations: 13.5 us -> 0.01 us
    reduce_scatter x1 -> x0, waiting for transfers between devices: 302 us -> none  [per_device(): lax.psum_scatter(partial_value, 'wide', scatter_dimension=1, tiled=True)]
    all_gather x1 -> x0, blocking collectives: 153 us -> none  [per_device(): row_block = lax.all_gather(coefficients, 'wide', axis=1, tiled=True)]
    scatter-add x2 -> x0, other arithmetic: 62.4 us -> none  [the longest x1 31.2 us: per_device(): partial_value = jnp.zeros((row_count, total_cols), jnp.float32).at[:, fla...]
    pallas_call x0 -> x1, Pallas kernels: none -> 59.1 us  [per_device(): pl.pallas_call(functools.partial(kernel, n), out_shape=jax.ShapeDtypeStru...]
    gather x6 -> x0, local copies, waits for them, and re-layouts: 31.8 us -> none  [the longest x3 15.9 us: per_device(): values = row_block[:, own_targets] * own_sign[None]]
    all_to_all x2 -> x0, starting transfers between devices: 26.7 us -> none  [the longest x1 19.6 us: per_device(): lax.all_to_all(row_block, 'tile', split_axis=1, concat_axis=0, tiled=True)]
    dot_general x4 -> x0, matrix products: 25.1 us -> none  [the longest x2 14.2 us: couple(): jnp.einsum('abq,pq->abp', spread, integrals, preferred_element_type=jnp.f...]
    all_to_all x2 -> x0, waiting for transfers between devices: 20.2 us -> none  [the longest x1 17.4 us: per_device(): lax.all_to_all(flipped, 'tile', split_axis=0, concat_axis=1, tiled=True)]
  transfers between devices with their start and end apart: 3 -> 0, of which waited for: 3 -> 0; matrix products, arithmetic and copies ran while one was open for 6% -> 0% of each run, Pallas kernels for 0% -> 0%
where the time goes in v3:
time: 60.7 us; the launch traced here: 60.5 us
  Pallas kernels  59.1 us (97%)
  local copies, waits for them, and re-layouts  1.35 us (2%)
    pallas_call x1, Pallas kernels, per_device(): pl.pallas_call(functools.partial(kernel, n), out_shape=jax.ShapeDtypeStru...  59.1 us
    unnamed x1, local copies, waits for them, and re-layouts  1.35 us

profile of v3, /device:TPU:1, one launch (start us, length us, event | category | flops | bytes accessed | tf_op | source)
XLA Modules:
  0.0 60.5 jit_solution(2908153148229182931)
XLA Ops:
  0.0 59.1 %sigma.1 = f32[48,96]{1,0:T(8,128)} custom-call(bf16[48,96]{1,0:T(8,128)(2,1)} %bitcast.3, bf16[400,400]{1,0:T(8,128)(2,1)} %integ.1, s32[110,1536]{1,0:T(8,128)} %tgt.1, s32[110,1536]{1,0:T(8,128)} %prs.1, s32[110,1536]{1,0:T(8,128)} %phs.1), custom_call_target="tpu_custom_call" | custom-call | tf_op jit(solution)/shard_map/sigma/pallas_call | solution.py:465
  59.1 1.3 %copy.7 = f32[96,48]{0,1:T(8,128)} copy(f32[96,48]{0,1:T(8,128)} %bitcast.2) | data formatting | bytes 36864

commit v4 on v3

--- a/solution.py
+++ b/solution.py
@@ -24,6 +24,7 @@
         xs=xs,
         ys=ys,
         zs=zs,
+        far=5 if zs == 8 else 1,
         spots=xs * ys,
         strings=strings,
         rows=strings // tiles,
@@ -40,9 +41,9 @@
 
 
 def kernel(n, coef, integ, tgt, prs, phs, out, raw, tabs, g_pad, p_part, c_pad, first, hold, gath_b, gath_a,
-           xt, x_all, t_all, w_all, u_all, part, xa, sb, rb, ob, sa, ra, sx, rx, oa, in_b, in_a, fin, fin_in,
-           s_tab, s1, r1, s2b, r2b, s5b, r5b, s2a, r2a, sxa, rxa, s5a, r5a, s6b, r6b, s6a, r6a,
-           s3b, r3b, s7, r7, s8, r8, s4, r4):
+           xt, x_all, t_all, w_all, u_all, part, xa, sb, rb, ob, sa, ra, sx, rx, oa, in_b, in_c, in_a, fin, fin_in,
+           s_tab, s1, r1, s2b, r2b, s5b, r5b, s2a, r2a, sxa, rxa, sxd, s5a, r5a, s6b, r6b, s6a, r6a,
+           s3b, r3b, s3c, r3c, s7, r7, s8, r8, s4, r4):
     bf16, f32 = jnp.bfloat16, jnp.float32
     tile, wide = lax.axis_index("tile"), lax.axis_index("wide")
     core, zl = lax.rem(tile, 2), tile // 2
@@ -58,6 +59,18 @@
 
     def on_line(z):
         return device(x, y, zh, z, core)
+
+    def on_mates_line(z):
+        return device(x_high * 2 + 1 - x_low, y, zh, z, core)
+
+    def at_spot_over(j):
+        return device(lax.rem(j, n.xs), j // n.xs, zh, zl, 1 - core)
+
+    def is_far(z):
+        return jnp.abs(z - zl) >= n.far
+
+    def near_first(i):
+        return jnp.where(zl < n.zs // 2, i, n.zs - 1 - i)
 
     def other(d):
         return lax.rem(spot + d, n.spots)
@@ -97,10 +110,12 @@
 
     def greet_line(d, carry):
         greet(on_line(other_z(d)))
+        greet(on_mates_line(other_z(d)))
         return carry
 
     def greet_plane(d, carry):
         greet(at_spot(other(d)))
+        greet(at_spot_over(other(d)))
         return carry
 
     greet(far_out)
@@ -160,13 +175,15 @@
         return carry
 
     builds = n.own // n.step
-    cut_a, cut_b = max(1, builds // 3), max(1, builds * 5 // 6)
-    lax.fori_loop(0, cut_a, build, 0)
-
-    pl.semaphore_wait(barrier, 2 + n.zs - 1 + n.spots - 1 + 1)
+    cuts = [0, builds // 3, builds * 2 // 3, builds * 5 // 6, builds]
+
+    pl.semaphore_wait(barrier, 2 + 2 * (n.zs - 1) + 2 * (n.spots - 1) + 1)
 
     def line(to, frm):
         return remote(first, gath_a.at[core, x_low, frm], s2a.at[to], r2a.at[frm], on_line(to))
+
+    def line_over(to):
+        return remote(first, gath_a.at[core, x_low, zl], sxd.at[to], rxa.at[zl], on_mates_line(to))
 
     def to_mate(z, side):
         ref = gath_a.at[core, side, z]
@@ -186,16 +203,25 @@
     forth = remote(first, hold, s1.at[0], r1.at[0], far_out)
     forth.start()
 
-    def start_line(d, carry):
-        line(other_z(d), zl).start()
-        return carry
-
-    lax.fori_loop(1, n.zs, start_line, 0)
+    def start_line(i, carry):
+        z = near_first(n.zs - 1 - i)
+
+        @pl.when(z != zl)
+        def _():
+            line(z, zl).start()
+
+        @pl.when(is_far(z))
+        def _():
+            line_over(z).start()
+
+        return carry
+
+    lax.fori_loop(0, n.zs, start_line, 0)
     gath_a[core, x_low, zl] = first[...]
     to_mate(zl, x_low).start()
     relay_a(zl, x_low, core).start()
 
-    lax.fori_loop(cut_a, cut_b, build, 0)
+    lax.fori_loop(cuts[0], cuts[1], build, 0)
 
     forth.wait_recv()
 
@@ -207,16 +233,25 @@
     gath_b[core, spot] = hold[...]
     relay_b(spot, core).start()
 
-    lax.fori_loop(cut_b, builds, build, 0)
-
-    def hand_line(d, carry):
-        z = other_z(d)
-        line(zl, z).wait_recv()
-        to_mate(z, x_low).start()
-        relay_a(z, x_low, core).start()
-        return carry
-
-    lax.fori_loop(1, n.zs, hand_line, 0)
+    lax.fori_loop(cuts[1], cuts[2], build, 0)
+
+    def hand_line(i, carry):
+        z = near_first(i)
+
+        @pl.when(z != zl)
+        def _():
+            line(zl, z).wait_recv()
+
+            @pl.when(jnp.logical_not(is_far(z)))
+            def _():
+                to_mate(z, x_low).start()
+
+            relay_a(z, x_low, core).start()
+
+        return carry
+
+    lax.fori_loop(0, n.zs, hand_line, 0)
+    lax.fori_loop(cuts[2], cuts[3], build, 0)
 
     def hand_plane(d, carry):
         j = other(d)
@@ -226,13 +261,14 @@
 
     lax.fori_loop(1, n.spots, hand_plane, 0)
 
-    def hand_mate(d, carry):
-        z = other_z(d)
+    def hand_mate(i, carry):
+        z = near_first(i)
         to_mate(z, 1 - x_low).wait_recv()
         relay_a(z, 1 - x_low, core).start()
         return carry
 
     lax.fori_loop(0, n.zs, hand_mate, 0)
+    lax.fori_loop(cuts[3], cuts[4], build, 0)
 
     def wait_relay_b(j, carry):
         relay_b(j, 1 - core).wait_recv()
@@ -319,11 +355,38 @@
     def to_plane(rows, to, frm):
         return remote(ob.at[rows], in_b.at[frm], s3b.at[to], r3b.at[frm], at_spot(to))
 
+    def to_plane_over(rows, to, frm):
+        return remote(ob.at[rows], in_c.at[frm], s3c.at[to], r3c.at[frm], at_spot_over(to))
+
+    def piece_rows(yy, cc, xx):
+        return pl.ds(pl.multiple_of(((yy * 2 + cc) * n.xs + xx) * n.cols, 16), n.cols)
+
+    last = n.order[-1]
+
     def scatter(h):
         at = slice(h * n.width, (h + 1) * n.width)
         part[:, at] = jnp.dot(u_all[...], t_all[:, at], preferred_element_type=f32)
 
     def sum_cores(h):
+        for kt in range(3 * h, 3 * h + 3):
+            at = slice(kt * LANES, (kt + 1) * LANES)
+            xt[at] = part[0:LANES, at].T
+        for yy in ys_of(h):
+            if h == last:
+                rows = pl.ds(yy * 2 * block, 2 * block)
+                ob[rows] = xt[rows].astype(bf16)
+                for i in range(n.xs):
+                    xx = lax.rem(x + i, n.xs)
+                    to_plane_over(piece_rows(yy, 1 - core, xx), yy * n.xs + xx, spot).start()
+
+                    @pl.when(jnp.logical_or(xx != x, y != yy))
+                    def _():
+                        to_plane(piece_rows(yy, core, xx), yy * n.xs + xx, spot).start()
+
+            else:
+                rows = block_rows(yy, 1 - core)
+                sb[rows] = xt[rows].astype(bf16)
+                cross_b(yy, 1 - core).start()
         t0, t1, t2 = (
             part[LANES : 2 * LANES, (3 * h + i) * LANES : (3 * h + i + 1) * LANES] for i in range(3)
         )
@@ -339,21 +402,9 @@
         for z in zs_of(h):
             sa[2 * z + 1 - core] = xa[2 * z + 1 - core].astype(bf16)
             cross_a(z, 1 - core).start()
-        for kt in range(3 * h, 3 * h + 3):
-            at = slice(kt * LANES, (kt + 1) * LANES)
-            xt[at] = part[0:LANES, at].T
-        for yy in ys_of(h):
-            rows = block_rows(yy, 1 - core)
-            sb[rows] = xt[rows].astype(bf16)
-            cross_b(yy, 1 - core).start()
 
     def sum_mates(h):
-        for z in zs_of(h):
-            cross_a(z, core).wait_recv()
-            xa[2 * z + core] = xa[2 * z + core] + ra[2 * z + core].astype(f32)
-            sx[z] = xa[2 * z + core, pass_on].astype(bf16)
-            across(z).start()
-        for yy in ys_of(h):
+        for yy in ys_of(h) if h != last else ():
             rows = block_rows(yy, core)
             cross_b(yy, core).wait_recv()
             total = xt[rows] + rb[rows].astype(f32)
@@ -361,11 +412,16 @@
             ob[rows] = total.astype(bf16)
             for i in range(n.xs):
                 xx = lax.rem(x + i, n.xs)
-                rows = pl.ds(pl.multiple_of(((yy * 2 + core) * n.xs + xx) * n.cols, 16), n.cols)
 
                 @pl.when(jnp.logical_or(xx != x, y != yy))
                 def _():
-                    to_plane(rows, yy * n.xs + xx, spot).start()
+                    to_plane(piece_rows(yy, core, xx), yy * n.xs + xx, spot).start()
+
+        for z in zs_of(h):
+            cross_a(z, core).wait_recv()
+            xa[2 * z + core] = xa[2 * z + core] + ra[2 * z + core].astype(f32)
+            sx[z] = xa[2 * z + core, pass_on].astype(bf16)
+            across(z).start()
 
     def sum_line(h):
         for z in zs_of(h):
@@ -388,8 +444,7 @@
         if i < n.ranges:
             sum_cores(n.order[i])
 
-    mine = pl.ds(pl.multiple_of(((y * 2 + core) * n.xs + x) * n.cols, 16), n.cols)
-    fin[...] = xt[mine]
+    fin[...] = xt[piece_rows(y, core, x)]
 
     def add_plane(d, carry):
         j = other(d)
@@ -398,6 +453,16 @@
         return carry
 
     lax.fori_loop(1, n.spots, add_plane, 0)
+
+    def add_over(j, carry):
+        to_plane_over(pl.ds(0, n.cols), spot, j).wait_recv()
+        fin[...] += in_c[j].astype(f32)
+        return carry
+
+    @pl.when((y >= ys_of(last)[0]) & (y <= ys_of(last)[-1]))
+    def _():
+        lax.fori_loop(0, n.spots, add_over, 0)
+
     back = remote(fin, fin_in, s4.at[0], r4.at[0], far_in)
     back.start()
 
@@ -417,12 +482,20 @@
         z = other_z(d)
         line(z, zl).wait_send()
         down_line(z, zl).wait_send()
+
+        @pl.when(is_far(z))
+        def _():
+            line_over(z).wait_send()
+
         return carry
 
     lax.fori_loop(1, n.zs, drain_line, 0)
 
     def drain_line_all(z, carry):
-        to_mate(z, x_low).wait_send()
+        @pl.when(jnp.logical_not(is_far(z)))
+        def _():
+            to_mate(z, x_low).wait_send()
+
         relay_a(z, 0, core).wait_send()
         relay_a(z, 1, core).wait_send()
         cross_a(z, 1 - core).wait_send()
@@ -445,7 +518,11 @@
 
     lax.fori_loop(0, n.spots, drain_plane_all, 0)
     for yy in range(n.ys):
-        cross_b(yy, 1 - core).wait_send()
+        if yy not in ys_of(last):
+            cross_b(yy, 1 - core).wait_send()
+            continue
+        for xx in range(n.xs):
+            to_plane_over(pl.ds(0, n.cols), yy * n.xs + xx, spot).wait_send()
 
     back.wait_recv()
     out[...] = c_pad[:, 0 : n.rows] + fin_in[:, 0 : n.rows]
@@ -493,6 +570,7 @@
             vmem((n.zs, *piece), bf16),
             vmem((n.zs, *piece), bf16),
             vmem((n.spots, *piece), bf16),
+            vmem((n.spots, *piece), bf16),
             vmem((n.zs, *piece), bf16),
             vmem(piece, f32),
             vmem(piece, f32),
@@ -507,12 +585,15 @@
             dma((n.zs,)),
             dma((n.zs,)),
             dma((n.zs,)),
+            dma((n.zs,)),
             dma((2, n.zs)),
             dma((2, n.zs)),
             dma((n.ys,)),
             dma((n.ys,)),
             dma((n.zs,)),
             dma((n.zs,)),
+            dma((n.spots,)),
+            dma((n.spots,)),
             dma((n.spots,)),
             dma((n.spots,)),
             dma((n.zs,)),

time: 60.7 us -> 63.7 us (1.049)
  Pallas kernels: 59.1 us -> 62.1 us
    pallas_call x1, Pallas kernels: 59.1 us -> 62.1 us  [per_device(): pl.pallas_call(functools.partial(kernel, n), out_shape=jax.ShapeDtypeStru...]
where the time goes in v4:
time: 63.7 us; the launch traced here: 63.5 us
  Pallas kernels  62.1 us (97%)
  local copies, waits for them, and re-layouts  1.35 us (2%)
    pallas_call x1, Pallas kernels, per_device(): pl.pallas_call(functools.partial(kernel, n), out_shape=jax.ShapeDtypeStru...  62.1 us
    unnamed x1, local copies, waits for them, and re-layouts  1.35 us

profile of v4, /device:TPU:1, one launch (start us, length us, event | category | flops | bytes accessed | tf_op | source)
XLA Modules:
  0.0 63.5 jit_solution(930794972008203104)
XLA Ops:
  0.0 62.1 %sigma.1 = f32[48,96]{1,0:T(8,128)} custom-call(bf16[48,96]{1,0:T(8,128)(2,1)} %bitcast.3, bf16[400,400]{1,0:T(8,128)(2,1)} %integ.1, s32[110,1536]{1,0:T(8,128)} %tgt.1, s32[110,1536]{1,0:T(8,128)} %prs.1, s32[110,1536]{1,0:T(8,128)} %phs.1), custom_call_target="tpu_custom_call" | custom-call | tf_op jit(solution)/shard_map/sigma/pallas_call | solution.py:542
  62.1 1.3 %copy.7 = f32[96,48]{0,1:T(8,128)} copy(f32[96,48]{0,1:T(8,128)} %bitcast.2) | data formatting | bytes 36864

commit v5 on v3

--- a/solution.py
+++ b/solution.py
@@ -24,6 +24,7 @@
         xs=xs,
         ys=ys,
         zs=zs,
+        group=zs // 2,
         spots=xs * ys,
         strings=strings,
         rows=strings // tiles,
@@ -40,9 +41,9 @@
 
 
 def kernel(n, coef, integ, tgt, prs, phs, out, raw, tabs, g_pad, p_part, c_pad, first, hold, gath_b, gath_a,
-           xt, x_all, t_all, w_all, u_all, part, xa, sb, rb, ob, sa, ra, sx, rx, oa, in_b, in_a, fin, fin_in,
-           s_tab, s1, r1, s2b, r2b, s5b, r5b, s2a, r2a, sxa, rxa, s5a, r5a, s6b, r6b, s6a, r6a,
-           s3b, r3b, s7, r7, s8, r8, s4, r4):
+           xt, x_all, t_all, w_all, u_all, part, xa, sb, rb, ob, sa, ra, sx, rx, oa, in_b, in_c, in_a, fin, fin_in,
+           s_tab, s1, r1, s2b, r2b, s5b, r5b, s2a, r2a, sxa, rxa, s2f, s2g, s5a, r5a, s6b, r6b, s6a, r6a,
+           s3b, r3b, s3c, r3c, s7, r7, s8, r8, s4, r4):
     bf16, f32 = jnp.bfloat16, jnp.float32
     tile, wide = lax.axis_index("tile"), lax.axis_index("wide")
     core, zl = lax.rem(tile, 2), tile // 2
@@ -58,6 +59,18 @@
 
     def on_line(z):
         return device(x, y, zh, z, core)
+
+    def on_mates_line(z):
+        return device(x_high * 2 + 1 - x_low, y, zh, z, core)
+
+    def at_spot_over(j):
+        return device(lax.rem(j, n.xs), j // n.xs, zh, zl, 1 - core)
+
+    def near_z(d):
+        return zl // n.group * n.group + lax.rem(zl + d, n.group)
+
+    def across_z(z):
+        return lax.rem(z + n.group, n.zs)
 
     def other(d):
         return lax.rem(spot + d, n.spots)
@@ -101,11 +114,17 @@
 
     def greet_plane(d, carry):
         greet(at_spot(other(d)))
+        greet(at_spot_over(other(d)))
         return carry
 
     greet(far_out)
     greet(far_in)
+    def greet_mates(d, carry):
+        greet(on_mates_line(near_z(d)))
+        return carry
+
     lax.fori_loop(1, n.zs, greet_line, 0)
+    lax.fori_loop(1, n.group, greet_mates, 0)
     lax.fori_loop(1, n.spots, greet_plane, 0)
     greet(partner)
 
@@ -160,13 +179,21 @@
         return carry
 
     builds = n.own // n.step
-    cut_a, cut_b = max(1, builds // 3), max(1, builds * 5 // 6)
-    lax.fori_loop(0, cut_a, build, 0)
-
-    pl.semaphore_wait(barrier, 2 + n.zs - 1 + n.spots - 1 + 1)
+    early = builds * 2 // 3
+
+    lax.fori_loop(0, early, build, 0)
+    pl.semaphore_wait(barrier, 2 + n.zs - 1 + n.group - 1 + 2 * (n.spots - 1) + 1)
 
     def line(to, frm):
         return remote(first, gath_a.at[core, x_low, frm], s2a.at[to], r2a.at[frm], on_line(to))
+
+    def line_on(to, frm):
+        ref = gath_a.at[core, x_low, frm]
+        return remote(ref, ref, s2f.at[to], r2a.at[frm], on_line(to))
+
+    def line_over(to, frm):
+        ref = gath_a.at[core, x_low, frm]
+        return remote(ref, ref, s2g.at[to], rxa.at[frm], on_mates_line(to))
 
     def to_mate(z, side):
         ref = gath_a.at[core, side, z]
@@ -187,15 +214,27 @@
     forth.start()
 
     def start_line(d, carry):
-        line(other_z(d), zl).start()
-        return carry
-
-    lax.fori_loop(1, n.zs, start_line, 0)
+        line(near_z(d), zl).start()
+        return carry
+
+    line(across_z(zl), zl).start()
+    lax.fori_loop(1, n.group, start_line, 0)
     gath_a[core, x_low, zl] = first[...]
     to_mate(zl, x_low).start()
     relay_a(zl, x_low, core).start()
 
-    lax.fori_loop(cut_a, cut_b, build, 0)
+    lax.fori_loop(early, builds, build, 0)
+
+    line(zl, across_z(zl)).wait_recv()
+
+    def start_line_on(d, carry):
+        line_on(near_z(d), across_z(zl)).start()
+        line_over(near_z(d), across_z(zl)).start()
+        return carry
+
+    lax.fori_loop(1, n.group, start_line_on, 0)
+    to_mate(across_z(zl), x_low).start()
+    relay_a(across_z(zl), x_low, core).start()
 
     forth.wait_recv()
 
@@ -207,16 +246,22 @@
     gath_b[core, spot] = hold[...]
     relay_b(spot, core).start()
 
-    lax.fori_loop(cut_b, builds, build, 0)
-
     def hand_line(d, carry):
-        z = other_z(d)
+        z = near_z(d)
         line(zl, z).wait_recv()
         to_mate(z, x_low).start()
         relay_a(z, x_low, core).start()
         return carry
 
-    lax.fori_loop(1, n.zs, hand_line, 0)
+    lax.fori_loop(1, n.group, hand_line, 0)
+
+    def hand_line_on(d, carry):
+        z = across_z(near_z(d))
+        line(zl, z).wait_recv()
+        relay_a(z, x_low, core).start()
+        return carry
+
+    lax.fori_loop(1, n.group, hand_line_on, 0)
 
     def hand_plane(d, carry):
         j = other(d)
@@ -318,6 +363,14 @@
 
     def to_plane(rows, to, frm):
         return remote(ob.at[rows], in_b.at[frm], s3b.at[to], r3b.at[frm], at_spot(to))
+
+    def to_plane_over(rows, to, frm):
+        return remote(ob.at[rows], in_c.at[frm], s3c.at[to], r3c.at[frm], at_spot_over(to))
+
+    def piece_rows(yy, cc, xx):
+        return pl.ds(pl.multiple_of(((yy * 2 + cc) * n.xs + xx) * n.cols, 16), n.cols)
+
+    last = n.order[-1]
 
     def scatter(h):
         at = slice(h * n.width, (h + 1) * n.width)
@@ -343,9 +396,21 @@
             at = slice(kt * LANES, (kt + 1) * LANES)
             xt[at] = part[0:LANES, at].T
         for yy in ys_of(h):
-            rows = block_rows(yy, 1 - core)
-            sb[rows] = xt[rows].astype(bf16)
-            cross_b(yy, 1 - core).start()
+            if h == last:
+                rows = pl.ds(yy * 2 * block, 2 * block)
+                ob[rows] = xt[rows].astype(bf16)
+                for i in range(n.xs):
+                    xx = lax.rem(x + i, n.xs)
+                    to_plane_over(piece_rows(yy, 1 - core, xx), yy * n.xs + xx, spot).start()
+
+                    @pl.when(jnp.logical_or(xx != x, y != yy))
+                    def _():
+                        to_plane(piece_rows(yy, core, xx), yy * n.xs + xx, spot).start()
+
+            else:
+                rows = block_rows(yy, 1 - core)
+                sb[rows] = xt[rows].astype(bf16)
+                cross_b(yy, 1 - core).start()
 
     def sum_mates(h):
         for z in zs_of(h):
@@ -353,7 +418,7 @@
             xa[2 * z + core] = xa[2 * z + core] + ra[2 * z + core].astype(f32)
             sx[z] = xa[2 * z + core, pass_on].astype(bf16)
             across(z).start()
-        for yy in ys_of(h):
+        for yy in ys_of(h) if h != last else ():
             rows = block_rows(yy, core)
             cross_b(yy, core).wait_recv()
             total = xt[rows] + rb[rows].astype(f32)
@@ -361,11 +426,10 @@
             ob[rows] = total.astype(bf16)
             for i in range(n.xs):
                 xx = lax.rem(x + i, n.xs)
-                rows = pl.ds(pl.multiple_of(((yy * 2 + core) * n.xs + xx) * n.cols, 16), n.cols)
 
                 @pl.when(jnp.logical_or(xx != x, y != yy))
                 def _():
-                    to_plane(rows, yy * n.xs + xx, spot).start()
+                    to_plane(piece_rows(yy, core, xx), yy * n.xs + xx, spot).start()
 
     def sum_line(h):
         for z in zs_of(h):
@@ -388,47 +452,69 @@
         if i < n.ranges:
             sum_cores(n.order[i])
 
-    mine = pl.ds(pl.multiple_of(((y * 2 + core) * n.xs + x) * n.cols, 16), n.cols)
-    fin[...] = xt[mine]
-
-    def add_plane(d, carry):
-        j = other(d)
-        to_plane(pl.ds(0, n.cols), spot, j).wait_recv()
-        fin[...] += in_b[j].astype(f32)
-        return carry
-
-    lax.fori_loop(1, n.spots, add_plane, 0)
+    in_b[spot] = jnp.zeros_like(first)
+
+    def wait_plane(d, carry):
+        to_plane(pl.ds(0, n.cols), spot, other(d)).wait_recv()
+        return carry
+
+    def wait_over(j, carry):
+        to_plane_over(pl.ds(0, n.cols), spot, j).wait_recv()
+        return carry
+
+    def total_of(ref, count):
+        terms = [ref[j].astype(f32) for j in range(count)]
+        while len(terms) > 1:
+            terms = [a + b for a, b in zip(terms[::2], terms[1::2])] + terms[len(terms) & ~1 :]
+        return terms[0]
+
+    in_last = (y >= ys_of(last)[0]) & (y <= ys_of(last)[-1])
+    lax.fori_loop(1, n.spots, wait_plane, 0)
+    fin[...] = xt[piece_rows(y, core, x)] + total_of(in_b, n.spots)
+
+    @pl.when(in_last)
+    def _():
+        lax.fori_loop(0, n.spots, wait_over, 0)
+        fin[...] += total_of(in_c, n.spots)
+
     back = remote(fin, fin_in, s4.at[0], r4.at[0], far_in)
     back.start()
 
-    c_pad[...] = xa[2 * zl + core, keep]
-
-    def add_line(d, carry):
-        z = other_z(d)
-        down_line(zl, z).wait_recv()
-        c_pad[...] += in_a[z].astype(f32)
-        return carry
-
-    lax.fori_loop(1, n.zs, add_line, 0)
+    in_a[zl] = jnp.zeros_like(first)
+
+    def wait_line(d, carry):
+        down_line(zl, other_z(d)).wait_recv()
+        return carry
+
+    lax.fori_loop(1, n.zs, wait_line, 0)
+    c_pad[...] = xa[2 * zl + core, keep] + total_of(in_a, n.zs)
 
     forth.wait_send()
 
     def drain_line(d, carry):
-        z = other_z(d)
+        down_line(other_z(d), zl).wait_send()
+        return carry
+
+    def drain_near(d, carry):
+        z = near_z(d)
         line(z, zl).wait_send()
-        down_line(z, zl).wait_send()
-        return carry
-
-    lax.fori_loop(1, n.zs, drain_line, 0)
+        line_on(z, zl).wait_send()
+        line_over(z, zl).wait_send()
+        to_mate(z, x_low).wait_send()
+        return carry
 
     def drain_line_all(z, carry):
-        to_mate(z, x_low).wait_send()
         relay_a(z, 0, core).wait_send()
         relay_a(z, 1, core).wait_send()
         cross_a(z, 1 - core).wait_send()
         across(z).wait_send()
         return carry
 
+    line(across_z(zl), zl).wait_send()
+    to_mate(zl, x_low).wait_send()
+    to_mate(across_z(zl), x_low).wait_send()
+    lax.fori_loop(1, n.zs, drain_line, 0)
+    lax.fori_loop(1, n.group, drain_near, 0)
     lax.fori_loop(0, n.zs, drain_line_all, 0)
 
     def drain_plane(d, carry):
@@ -445,7 +531,11 @@
 
     lax.fori_loop(0, n.spots, drain_plane_all, 0)
     for yy in range(n.ys):
-        cross_b(yy, 1 - core).wait_send()
+        if yy not in ys_of(last):
+            cross_b(yy, 1 - core).wait_send()
+            continue
+        for xx in range(n.xs):
+            to_plane_over(pl.ds(0, n.cols), yy * n.xs + xx, spot).wait_send()
 
     back.wait_recv()
     out[...] = c_pad[:, 0 : n.rows] + fin_in[:, 0 : n.rows]
@@ -493,6 +583,7 @@
             vmem((n.zs, *piece), bf16),
             vmem((n.zs, *piece), bf16),
             vmem((n.spots, *piece), bf16),
+            vmem((n.spots, *piece), bf16),
             vmem((n.zs, *piece), bf16),
             vmem(piece, f32),
             vmem(piece, f32),
@@ -507,12 +598,16 @@
             dma((n.zs,)),
             dma((n.zs,)),
             dma((n.zs,)),
+            dma((n.zs,)),
+            dma((n.zs,)),
             dma((2, n.zs)),
             dma((2, n.zs)),
             dma((n.ys,)),
             dma((n.ys,)),
             dma((n.zs,)),
             dma((n.zs,)),
+            dma((n.spots,)),
+            dma((n.spots,)),
             dma((n.spots,)),
             dma((n.spots,)),
             dma((n.zs,)),

time: 60.7 us -> 65.2 us (1.074)
  Pallas kernels: 59.1 us -> 63.6 us
    pallas_call x1, Pallas kernels: 59.1 us -> 63.6 us  [per_device(): pl.pallas_call(functools.partial(kernel, n), out_shape=jax.ShapeDtypeStru...]
where the time goes in v5:
time: 65.2 us; the launch traced here: 65 us
  Pallas kernels  63.6 us (98%)
  local copies, waits for them, and re-layouts  1.35 us (2%)
    pallas_call x1, Pallas kernels, per_device(): pl.pallas_call(functools.partial(kernel, n), out_shape=jax.ShapeDtypeStru...  63.6 us
    unnamed x1, local copies, waits for them, and re-layouts  1.35 us

profile of v5, /device:TPU:1, one launch (start us, length us, event | category | flops | bytes accessed | tf_op | source)
XLA Modules:
  0.0 65.0 jit_solution(355859211218674294)
XLA Ops:
  0.0 63.6 %sigma.1 = f32[48,96]{1,0:T(8,128)} custom-call(bf16[48,96]{1,0:T(8,128)(2,1)} %bitcast.3, bf16[400,400]{1,0:T(8,128)(2,1)} %integ.1, s32[110,1536]{1,0:T(8,128)} %tgt.1, s32[110,1536]{1,0:T(8,128)} %prs.1, s32[110,1536]{1,0:T(8,128)} %phs.1), custom_call_target="tpu_custom_call" | custom-call | tf_op jit(solution)/shard_map/sigma/pallas_call | solution.py:555
  63.6 1.3 %copy.7 = f32[96,48]{0,1:T(8,128)} copy(f32[96,48]{0,1:T(8,128)} %bitcast.2) | data formatting | bytes 36864

commit v6 on v5

--- a/solution.py
+++ b/solution.py
@@ -24,7 +24,7 @@
         xs=xs,
         ys=ys,
         zs=zs,
-        group=zs // 2,
+        far=99,
         spots=xs * ys,
         strings=strings,
         rows=strings // tiles,
@@ -42,7 +42,7 @@
 
 def kernel(n, coef, integ, tgt, prs, phs, out, raw, tabs, g_pad, p_part, c_pad, first, hold, gath_b, gath_a,
            xt, x_all, t_all, w_all, u_all, part, xa, sb, rb, ob, sa, ra, sx, rx, oa, in_b, in_c, in_a, fin, fin_in,
-           s_tab, s1, r1, s2b, r2b, s5b, r5b, s2a, r2a, sxa, rxa, s2f, s2g, s5a, r5a, s6b, r6b, s6a, r6a,
+           s_tab, s1, r1, s2b, r2b, s5b, r5b, s2a, r2a, sxa, rxa, sxd, s5a, r5a, s6b, r6b, s6a, r6a,
            s3b, r3b, s3c, r3c, s7, r7, s8, r8, s4, r4):
     bf16, f32 = jnp.bfloat16, jnp.float32
     tile, wide = lax.axis_index("tile"), lax.axis_index("wide")
@@ -66,11 +66,11 @@
     def at_spot_over(j):
         return device(lax.rem(j, n.xs), j // n.xs, zh, zl, 1 - core)
 
-    def near_z(d):
-        return zl // n.group * n.group + lax.rem(zl + d, n.group)
-
-    def across_z(z):
-        return lax.rem(z + n.group, n.zs)
+    def is_far(z):
+        return jnp.abs(z - zl) >= n.far
+
+    def near_first(i):
+        return jnp.where(zl < n.zs // 2, i, n.zs - 1 - i)
 
     def other(d):
         return lax.rem(spot + d, n.spots)
@@ -119,12 +119,7 @@
 
     greet(far_out)
     greet(far_in)
-    def greet_mates(d, carry):
-        greet(on_mates_line(near_z(d)))
-        return carry
-
     lax.fori_loop(1, n.zs, greet_line, 0)
-    lax.fori_loop(1, n.group, greet_mates, 0)
     lax.fori_loop(1, n.spots, greet_plane, 0)
     greet(partner)
 
@@ -179,21 +174,16 @@
         return carry
 
     builds = n.own // n.step
-    early = builds * 2 // 3
-
-    lax.fori_loop(0, early, build, 0)
-    pl.semaphore_wait(barrier, 2 + n.zs - 1 + n.group - 1 + 2 * (n.spots - 1) + 1)
+    cuts = [2, 4, 6, 6, 6]
+
+    lax.fori_loop(0, 2, build, 0)
+    pl.semaphore_wait(barrier, 2 + (n.zs - 1) + 2 * (n.spots - 1) + 1)
 
     def line(to, frm):
         return remote(first, gath_a.at[core, x_low, frm], s2a.at[to], r2a.at[frm], on_line(to))
 
-    def line_on(to, frm):
-        ref = gath_a.at[core, x_low, frm]
-        return remote(ref, ref, s2f.at[to], r2a.at[frm], on_line(to))
-
-    def line_over(to, frm):
-        ref = gath_a.at[core, x_low, frm]
-        return remote(ref, ref, s2g.at[to], rxa.at[frm], on_mates_line(to))
+    def line_over(to):
+        return remote(first, gath_a.at[core, x_low, zl], sxd.at[to], rxa.at[zl], on_mates_line(to))
 
     def to_mate(z, side):
         ref = gath_a.at[core, side, z]
@@ -214,27 +204,15 @@
     forth.start()
 
     def start_line(d, carry):
-        line(near_z(d), zl).start()
-        return carry
-
-    line(across_z(zl), zl).start()
-    lax.fori_loop(1, n.group, start_line, 0)
+        line(other_z(d), zl).start()
+        return carry
+
+    lax.fori_loop(1, n.zs, start_line, 0)
     gath_a[core, x_low, zl] = first[...]
     to_mate(zl, x_low).start()
     relay_a(zl, x_low, core).start()
 
-    lax.fori_loop(early, builds, build, 0)
-
-    line(zl, across_z(zl)).wait_recv()
-
-    def start_line_on(d, carry):
-        line_on(near_z(d), across_z(zl)).start()
-        line_over(near_z(d), across_z(zl)).start()
-        return carry
-
-    lax.fori_loop(1, n.group, start_line_on, 0)
-    to_mate(across_z(zl), x_low).start()
-    relay_a(across_z(zl), x_low, core).start()
+    lax.fori_loop(cuts[0], cuts[1], build, 0)
 
     forth.wait_recv()
 
@@ -246,22 +224,16 @@
     gath_b[core, spot] = hold[...]
     relay_b(spot, core).start()
 
+    lax.fori_loop(cuts[1], cuts[2], build, 0)
+
     def hand_line(d, carry):
-        z = near_z(d)
+        z = other_z(d)
         line(zl, z).wait_recv()
         to_mate(z, x_low).start()
         relay_a(z, x_low, core).start()
         return carry
 
-    lax.fori_loop(1, n.group, hand_line, 0)
-
-    def hand_line_on(d, carry):
-        z = across_z(near_z(d))
-        line(zl, z).wait_recv()
-        relay_a(z, x_low, core).start()
-        return carry
-
-    lax.fori_loop(1, n.group, hand_line_on, 0)
+    lax.fori_loop(1, n.zs, hand_line, 0)
 
     def hand_plane(d, carry):
         j = other(d)
@@ -278,6 +250,7 @@
         return carry
 
     lax.fori_loop(0, n.zs, hand_mate, 0)
+    lax.fori_loop(cuts[3], cuts[4], build, 0)
 
     def wait_relay_b(j, carry):
         relay_b(j, 1 - core).wait_recv()
@@ -318,7 +291,7 @@
             at = (3 * four + i) * LANES
             x_all[LANES : 2 * LANES, at : at + LANES] = value.astype(bf16)
 
-    many = min(8, n.own)
+    many = min(16, n.own)
 
     def couple(it, carry):
         rows = pl.ds(pl.multiple_of(it * many * LANES, many * LANES), many * LANES)
@@ -492,29 +465,29 @@
     forth.wait_send()
 
     def drain_line(d, carry):
-        down_line(other_z(d), zl).wait_send()
-        return carry
-
-    def drain_near(d, carry):
-        z = near_z(d)
+        z = other_z(d)
         line(z, zl).wait_send()
-        line_on(z, zl).wait_send()
-        line_over(z, zl).wait_send()
-        to_mate(z, x_low).wait_send()
-        return carry
+        down_line(z, zl).wait_send()
+
+        @pl.when(is_far(z))
+        def _():
+            line_over(z).wait_send()
+
+        return carry
+
+    lax.fori_loop(1, n.zs, drain_line, 0)
 
     def drain_line_all(z, carry):
+        @pl.when(jnp.logical_not(is_far(z)))
+        def _():
+            to_mate(z, x_low).wait_send()
+
         relay_a(z, 0, core).wait_send()
         relay_a(z, 1, core).wait_send()
         cross_a(z, 1 - core).wait_send()
         across(z).wait_send()
         return carry
 
-    line(across_z(zl), zl).wait_send()
-    to_mate(zl, x_low).wait_send()
-    to_mate(across_z(zl), x_low).wait_send()
-    lax.fori_loop(1, n.zs, drain_line, 0)
-    lax.fori_loop(1, n.group, drain_near, 0)
     lax.fori_loop(0, n.zs, drain_line_all, 0)
 
     def drain_plane(d, carry):
@@ -599,7 +572,6 @@
             dma((n.zs,)),
             dma((n.zs,)),
             dma((n.zs,)),
-            dma((n.zs,)),
             dma((2, n.zs)),
             dma((2, n.zs)),
             dma((n.ys,)),

time: 65.2 us -> 59.9 us (0.919)
  Pallas kernels: 63.6 us -> 58.3 us
    pallas_call x1, Pallas kernels: 63.6 us -> 58.3 us  [per_device(): pl.pallas_call(functools.partial(kernel, n), out_shape=jax.ShapeDtypeStru...]
where the time goes in v6:
time: 59.9 us; the launch traced here: 59.6 us
  Pallas kernels  58.3 us (97%)
  local copies, waits for them, and re-layouts  1.35 us (2%)
    pallas_call x1, Pallas kernels, per_device(): pl.pallas_call(functools.partial(kernel, n), out_shape=jax.ShapeDtypeStru...  58.3 us
    unnamed x1, local copies, waits for them, and re-layouts  1.35 us

profile of v6, /device:TPU:1, one launch (start us, length us, event | category | flops | bytes accessed | tf_op | source)
XLA Modules:
  0.0 59.6 jit_solution(4576695207207962965)
XLA Ops:
  0.0 58.3 %sigma.1 = f32[48,96]{1,0:T(8,128)} custom-call(bf16[48,96]{1,0:T(8,128)(2,1)} %bitcast.3, bf16[400,400]{1,0:T(8,128)(2,1)} %integ.1, s32[110,1536]{1,0:T(8,128)} %tgt.1, s32[110,1536]{1,0:T(8,128)} %prs.1, s32[110,1536]{1,0:T(8,128)} %phs.1), custom_call_target="tpu_custom_call" | custom-call | tf_op jit(solution)/shard_map/sigma/pallas_call | solution.py:528
  58.3 1.3 %copy.7 = f32[96,48]{0,1:T(8,128)} copy(f32[96,48]{0,1:T(8,128)} %bitcast.2) | data formatting | bytes 36864

commit v7 on v6

--- a/solution.py
+++ b/solution.py
@@ -35,7 +35,7 @@
         pair_pad=-(-pair_count // LANES) * LANES,
         step=8,
         ranges=ranges,
-        order=sorted(range(ranges), key=lambda h: -abs(2 * h - ranges + 1)),
+        groups=((0, 1), (3,), (2,)) if ranges == 4 else tuple((h,) for h in range(ranges)),
         width=strings // ranges,
     )
 
@@ -291,7 +291,7 @@
             at = (3 * four + i) * LANES
             x_all[LANES : 2 * LANES, at : at + LANES] = value.astype(bf16)
 
-    many = min(16, n.own)
+    many = min(24, n.own)
 
     def couple(it, carry):
         rows = pl.ds(pl.multiple_of(it * many * LANES, many * LANES), many * LANES)
@@ -343,10 +343,10 @@
     def piece_rows(yy, cc, xx):
         return pl.ds(pl.multiple_of(((yy * 2 + cc) * n.xs + xx) * n.cols, 16), n.cols)
 
-    last = n.order[-1]
-
-    def scatter(h):
-        at = slice(h * n.width, (h + 1) * n.width)
+    last = n.groups[-1][-1]
+
+    def scatter(group):
+        at = slice(group[0] * n.width, (group[-1] + 1) * n.width)
         part[:, at] = jnp.dot(u_all[...], t_all[:, at], preferred_element_type=f32)
 
     def sum_cores(h):
@@ -415,15 +415,16 @@
             def _():
                 down_line(z, zl).start()
 
-    for i in range(n.ranges + 2):
-        if i < n.ranges:
-            scatter(n.order[i])
-        if 0 <= i - 2 < n.ranges:
-            sum_line(n.order[i - 2])
-        if 0 <= i - 1 < n.ranges:
-            sum_mates(n.order[i - 1])
-        if i < n.ranges:
-            sum_cores(n.order[i])
+    count = len(n.groups)
+    for i in range(count + 2):
+        if i < count:
+            scatter(n.groups[i])
+        for h in n.groups[i - 2] if 0 <= i - 2 < count else ():
+            sum_line(h)
+        for h in n.groups[i - 1] if 0 <= i - 1 < count else ():
+            sum_mates(h)
+        for h in n.groups[i] if i < count else ():
+            sum_cores(h)
 
     in_b[spot] = jnp.zeros_like(first)
 

time: 59.9 us -> 61.2 us (1.022)
  Pallas kernels: 58.3 us -> 59.6 us
    pallas_call x1, Pallas kernels: 58.3 us -> 59.6 us  [per_device(): pl.pallas_call(functools.partial(kernel, n), out_shape=jax.ShapeDtypeStru...]
where the time goes in v7:
time: 61.2 us; the launch traced here: 61 us
  Pallas kernels  59.6 us (97%)
  local copies, waits for them, and re-layouts  1.35 us (2%)
    pallas_call x1, Pallas kernels, per_device(): pl.pallas_call(functools.partial(kernel, n), out_shape=jax.ShapeDtypeStru...  59.6 us
    unnamed x1, local copies, waits for them, and re-layouts  1.35 us

profile of v7, /device:TPU:1, one launch (start us, length us, event | category | flops | bytes accessed | tf_op | source)
XLA Modules:
  0.0 61.0 jit_solution(6958627184776562963)
XLA Ops:
  0.0 59.6 %sigma.1 = f32[48,96]{1,0:T(8,128)} custom-call(bf16[48,96]{1,0:T(8,128)(2,1)} %bitcast.3, bf16[400,400]{1,0:T(8,128)(2,1)} %integ.1, s32[110,1536]{1,0:T(8,128)} %tgt.1, s32[110,1536]{1,0:T(8,128)} %prs.1, s32[110,1536]{1,0:T(8,128)} %phs.1), custom_call_target="tpu_custom_call" | custom-call | tf_op jit(solution)/shard_map/sigma/pallas_call | solution.py:529
  59.6 1.3 %copy.7 = f32[96,48]{0,1:T(8,128)} copy(f32[96,48]{0,1:T(8,128)} %bitcast.2) | data formatting | bytes 36864
